TPU v7x, 1024 devices: a whole 4x4x32 slice. The times are simulated.
1024 devices in a mesh: outer: 4 (over y), tensor: 64 (over z, core), rep: 4 (over x).
Axes of the slice: x: 4, y: 4, z: 32, core: 2. Of those that a mesh axis runs over, the one named last changes fastest.
Arguments:
- master: float32 [64, 112, 128, 128], P('tensor', ('outer', 'rep')), may hold values from -80 to 80
- synced: bfloat16 [64, 112, 128, 128], P('tensor', ('outer', 'rep')), may hold values from -6 to 6
- keep_mask: int32 [64, 112], P('tensor', ('outer', 'rep')), may hold values from 0 to 1, as said below
- resident: bfloat16 [2, 8192, 7168], P(None, 'tensor'), may hold values from -6 to 6
Outputs:
- updated: bfloat16 [2, 8192, 7168], P(None, 'tensor')
Inputs may be any that keep to these rules, and one draw needn't show every extreme that they name: `keep_mask`: within one learner shard's block of 7 tiles of one head (aligned blocks along the second dimension) at most 4 are listed, and some block lists exactly 4.
All inputs are finite; a program needn't handle non-finite values.
Results may differ from a plain program's by a relative error of at most 0.0025.
Values may be sent and summed in bfloat16 or wider, within the bound.
No kernel may reach another device: no remote copies, remote signals or barrier semaphores. Data moves between devices by JAX's collectives and lax.ppermute only.
A program may use at most 64 MiB of HBM per device.

v0:
```python
import math

import jax
import jax.numpy as jnp
from jax import lax
from jax.sharding import PartitionSpec as P


def body(master, synced, keep_mask, resident):
    heads_here, tile_count, tile_side, _ = master.shape
    difference = (master - synced.astype(jnp.float32)).astype(jnp.bfloat16)
    listed_delta = difference * keep_mask.astype(jnp.bfloat16)[:, :, None, None]
    widened = listed_delta.astype(jnp.float32)
    squares = jnp.sum(widened * widened)
    total = lax.psum(squares, ("outer", "tensor", "rep"))
    devices_all = lax.axis_size("outer") * lax.axis_size("tensor") * lax.axis_size("rep")
    limit = 0.25 * tile_side * math.sqrt(heads_here * tile_count * devices_all)
    factor = jnp.minimum(jnp.float32(1.0), limit / jnp.sqrt(total))
    assembled = lax.all_gather(listed_delta, ("outer", "rep"), axis=1, tiled=True).astype(
        jnp.float32
    )
    layers, rows_here, width = resident.shape
    row_tiles = rows_here // (heads_here * tile_side)
    arranged = assembled.reshape(
        heads_here, layers, row_tiles, width // tile_side, tile_side, tile_side
    )
    arranged = arranged.transpose(1, 0, 2, 4, 3, 5).reshape(layers, rows_here, width)
    return (resident.astype(jnp.float32) + factor * arranged).astype(jnp.bfloat16)


def solution(mesh):
    placed = (
        P("tensor", ("outer", "rep"), None, None),
        P("tensor", ("outer", "rep"), None, None),
        P("tensor", ("outer", "rep")),
        P(None, "tensor", None),
    )
    return jax.shard_map(
        body, mesh=mesh, in_specs=placed, out_specs=P(None, "tensor", None), check_vma=False
    )
```

profile of v0, /device:TPU:1, one launch (start us, length us, event | category | flops | bytes accessed | tf_op | source)
XLA Modules:
  0.0 213.4 jit_solution(16655355616167003044)
XLA Ops:
  6.5 0.0 all-gather.2.cloned.1.call-start
  6.5 0.7 convert_bitcast_fusion
  7.2 2.6 %multiply_reduce_fusion = (f32[]{:T(128)}, bf16[1,7,128,128]{3,2,0,1:T(8,128)(2,1)}) fusion(bf16[7]{0:T(256)(128)(2,1)S(1)} %convert_bitcast_fusion, bf16[1,7,128,128]{3,2,1,0:T(8,128)(2,1)} %param.5, f32[1,7,128,128]{3,2,1,0:T(8,128)} %param.4), kind=kLoop, calls=%fused_computation.4 | loop fusion | flops 802815 | bytes 917522 | tf_op jit(solution)/shard_map/reduce_sum | solution.py:14
  9.7 0.0 all-gather.2.cloned.1.call-update
  9.8 170.5 %psum.7 = f32[]{:T(128)} all-reduce(f32[]{:T(128)} %get-tuple-element.5), channel_id=1, replica_groups=mesh['outer'=4,'tensor'=64,'rep'=4] {'outer','tensor','rep'}, use_global_device_ids=true, to_apply=%region_1.0 | all-reduce | flops 1 | bytes 8 | tf_op jit(solution)/shard_map/psum | solution.py:15
  181.0 0.0 all-gather.2.cloned.1.call-done
  181.0 3.0 %convert_multiply_fusion = f32[1,112,128,128]{3,2,0,1:T(8,128)S(1)} fusion(bf16[1,112,128,128]{3,2,0,1:T(8,128)(2,1)} %all-gather.2.cloned.1.call-done, f32[]{:T(128)S(6)} %min_shard_map.3), kind=kLoop, calls=%fused_computation.1 | loop fusion | flops 3670016 | bytes 11010052 | tf_op jit(solution)/shard_map/mul | solution.py:28
  184.1 7.2 %copy.8 = f32[2,1,1,128,56,128]{5,4,3,0,2,1:T(8,128)} copy(f32[2,1,1,128,56,128]{5,3,4,0,2,1:T(8,128)S(1)} %bitcast.19) | data formatting | bytes 14680064 | tf_op jit(solution)/shard_map/mul | solution.py:28
  191.3 8.3 %mul.36 = f32[2,128,7168]{2,1,0:T(8,128)} reshape(f32[2,1,1,128,56,128]{5,4,3,0,2,1:T(8,128)} %copy.8) | data formatting | bytes 14680064 | tf_op jit(solution)/shard_map/mul | solution.py:28
  199.6 6.9 %add_convert_fusion = bf16[2,128,7168]{2,1,0:T(8,128)(2,1)} fusion(f32[2,128,7168]{2,1,0:T(8,128)} %mul.36, bf16[2,128,7168]{2,1,0:T(8,128)(2,1)} %param.7), kind=kLoop, calls=%fused_computation | loop fusion | flops 5505024 | bytes 14680064 | tf_op jit(solution)/shard_map/convert_element_type | solution.py:28
Async XLA Ops:
  6.5 174.5 %all-gather.2.cloned.1.call-start = ((), (), s32[]{:S(2)}) async-start(), calls=%async_computation | async-start | bytes 3899392 | tf_op jit(solution)/shard_map/all_gather | solution.py:19
Sparse Core Ops, SparseCore 0:
  11.5 93.4 all-gather.1
where the time goes:
time: 214 us; the launch traced here: 213 us
  blocking collectives  170 us (79%)
  local copies, waits for them, and re-layouts  15.5 us (7%)
  between operations  14.1 us (7%)
  other arithmetic  13.2 us (6%)
    psum x1, blocking collectives, body(): total = lax.psum(squares, ('outer', 'tensor', 'rep'))  170 us
    mul x2, local copies, waits for them, and re-layouts, body(): factor * arranged  15.5 us
    convert_element_type x1, other arithmetic, body(): (resident.astype(jnp.float32) + factor * arranged).astype(jnp.bfloat16)  6.93 us
  transfers between devices with their start and end apart: 1, of which 0 were waited for; matrix products, arithmetic and copies ran while one was open for 0% of the time, Pallas kernels for 0%

commit v1 on v0

v1 whole, which is shorter than its diff:
```python
import functools
import math

import jax
import jax.numpy as jnp
from jax import lax
from jax.experimental import pallas as pl
from jax.experimental.pallas import tpu as pltpu
from jax.sharding import Mesh, PartitionSpec as P

SLOTS = 4
TILE = 128


def pick_kernel(mask_ref, master_ref, synced_ref, tiles_ref, note_ref):
    count = mask_ref.shape[1]
    lane = lax.broadcasted_iota(jnp.int32, note_ref.shape[1:], 1)
    note = jnp.zeros(note_ref.shape[1:], jnp.float32)
    where = [jnp.int32(0)] * SLOTS
    used = jnp.int32(0)
    for i in range(count):
        listed = mask_ref[0, i] > 0
        for s in range(SLOTS):
            where[s] = jnp.where(listed & (used == s), i, where[s])
        slot = jnp.where(listed, used, -1)
        note = jnp.where(lane == 1 + i, slot.astype(jnp.float32), note)
        used = used + listed.astype(jnp.int32)
    squares = jnp.zeros((8, TILE), jnp.float32)
    for s in range(SLOTS):
        delta = (master_ref[0, where[s]] - synced_ref[0, where[s]].astype(jnp.float32)).astype(jnp.bfloat16)
        tiles_ref[s] = delta
        wide = jnp.where(used > s, delta.astype(jnp.float32), 0.0)
        squares = squares + jnp.sum((wide * wide).reshape(-1, 8, TILE), axis=0)
    note = jnp.where(lane == 0, jnp.sum(squares), note)
    note_ref[...] = jnp.broadcast_to(note[None], note_ref.shape)


def plane_kernel(outers, reps, notes_ref, sums_ref, table_ref):
    core = lax.axis_index("core")
    rows = notes_ref[:, 0, :]
    lane = lax.broadcasted_iota(jnp.int32, rows.shape, 1)
    total = jnp.sum(jnp.where(lane == 0, rows, 0.0))
    sums_ref[...] = jnp.full(sums_ref.shape, total, jnp.float32)
    for y in range(outers):
        mine = notes_ref[pl.ds((y * 2 + core) * reps, reps), 0, :]
        table_ref[y * reps:(y + 1) * reps, :] = mine.astype(jnp.int32)


def apply_kernel(limit, count, table_ref, sums_ref, tiles_ref, resident_ref, out_ref):
    shard = pl.program_id(0)
    total = jnp.sum(sums_ref[:, 0:1, :], axis=0)
    factor = jnp.minimum(jnp.float32(1.0), limit / jnp.sqrt(total))
    out_ref[...] = resident_ref[...]
    for i in range(count):
        slot = table_ref[shard, 1 + i]

        @pl.when(slot >= 0)
        def _():
            cols = slice(i * TILE, (i + 1) * TILE)
            moved = factor * tiles_ref[slot].astype(jnp.float32)
            out_ref[0, :, cols] = (resident_ref[0, :, cols].astype(jnp.float32) + moved).astype(jnp.bfloat16)


def body(master, synced, keep_mask, resident):
    outers, chips, cores, reps = (lax.axis_size(a) for a in ("outer", "z", "core", "rep"))
    _, count, side, _ = master.shape
    layers, rows, width = resident.shape
    shards = outers * reps
    plane = shards * cores
    vmem = pl.BlockSpec(memory_space=pltpu.VMEM)
    smem = pl.BlockSpec(memory_space=pltpu.SMEM)
    with jax.named_scope("pick"):
        tiles, notes = pl.pallas_call(
            pick_kernel,
            out_shape=(
                jax.ShapeDtypeStruct((SLOTS, side, side), jnp.bfloat16),
                jax.ShapeDtypeStruct((plane, 8, TILE), jnp.float32),
            ),
            in_specs=[smem, vmem, vmem],
            out_specs=(vmem, vmem),
        )(keep_mask, master, synced)
    with jax.named_scope("gather"):
        gathered = lax.all_gather(tiles, ("outer", "rep"), axis=0, tiled=True)
    with jax.named_scope("plane_sum"):
        notes = lax.all_to_all(notes, ("outer", "core", "rep"), 0, 0, tiled=True)
        sums, table = pl.pallas_call(
            functools.partial(plane_kernel, outers, reps),
            out_shape=(
                jax.ShapeDtypeStruct((chips, 8, TILE), jnp.float32),
                jax.ShapeDtypeStruct((shards, TILE), jnp.int32),
            ),
            in_specs=[vmem],
            out_specs=(vmem, vmem),
        )(notes)
    with jax.named_scope("z_sum"):
        sums = lax.all_to_all(sums, "z", 0, 0, tiled=True)
    limit = 0.25 * side * math.sqrt(count * plane * chips)
    per_layer = width // (count * side)
    place = pl.BlockSpec((1, rows, count * side), lambda j, t: (j // per_layer, 0, j % per_layer))
    with jax.named_scope("apply"):
        return pl.pallas_call(
            functools.partial(apply_kernel, limit, count),
            out_shape=jax.ShapeDtypeStruct(resident.shape, resident.dtype),
            grid_spec=pltpu.PrefetchScalarGridSpec(
                num_scalar_prefetch=1,
                grid=(shards,),
                in_specs=[
                    pl.BlockSpec((chips, 8, TILE), lambda j, t: (0, 0, 0)),
                    pl.BlockSpec((SLOTS, side, side), lambda j, t: (j, 0, 0)),
                    place,
                ],
                out_specs=place,
            ),
        )(table, sums, gathered, resident)


def solution(mesh):
    outers, tensors, reps = mesh.devices.shape
    fine = Mesh(mesh.devices.reshape(outers, tensors // 2, 2, reps), ("outer", "z", "core", "rep"))
    head = ("z", "core")
    placed = (
        P(head, ("outer", "rep"), None, None),
        P(head, ("outer", "rep"), None, None),
        P(head, ("outer", "rep")),
        P(None, head, None),
    )
    return jax.shard_map(
        body, mesh=fine, in_specs=placed, out_specs=P(None, head, None), check_vma=False
    )
```

time: 214 us -> 119 us (0.56)
  blocking collectives: 170 us -> 74.7 us
  Pallas kernels: 0 us -> 15.8 us
  local copies, waits for them, and re-layouts: 15.5 us -> 0 us
  waiting for transfers between devices: 0.04 us -> 15 us
  other arithmetic: 13.2 us -> 0 us
    psum x1 -> x0, blocking collectives: 170 us -> none  [body(): total = lax.psum(squares, ('outer', 'tensor', 'rep'))]
    all_to_all x0 -> x2, blocking collectives: none -> 74.7 us  [the longest x1 48.6 us: body(): sums = lax.all_to_all(sums, 'z', 0, 0, tiled=True)]
    pallas_call x0 -> x3, Pallas kernels: none -> 15.8 us  [the longest x1 12.1 us: body(): pl.pallas_call(functools.partial(apply_kernel, limit, count), out_shape=j...]
    mul x2 -> x0, local copies, waits for them, and re-layouts: 15.5 us -> none  [body(): factor * arranged]
    all_gather x1, waiting for transfers between devices: 0.02 us -> 15 us  [body(): gathered = lax.all_gather(tiles, ('outer', 'rep'), axis=0, tiled=True)]
    convert_element_type x1 -> x0, other arithmetic: 6.93 us -> none  [body(): (resident.astype(jnp.float32) + factor * arranged).astype(jnp.bfloat16)]
    mul x2 -> x0, other arithmetic: 3.71 us -> none  [the longest x1 3.05 us: body(): factor * arranged]
    reduce_sum x1 -> x0, other arithmetic: 2.55 us -> none  [body(): squares = jnp.sum(widened * widened)]
  transfers between devices with their start and end apart: 1 -> 1, of which waited for: 0 -> 1; matrix products, arithmetic and copies ran while one was open for 0% -> 0% of each run, Pallas kernels for 0% -> 1%
where the time goes in v1:
time: 119 us
  blocking collectives  74.7 us (63%)
  Pallas kernels  15.8 us (13%)
  waiting for transfers between devices  15 us (13%)
  between operations  13.4 us (11%)
    all_to_all x1, blocking collectives, body(): sums = lax.all_to_all(sums, 'z', 0, 0, tiled=True)  48.6 us
    all_to_all x1, blocking collectives, body(): notes = lax.all_to_all(notes, ('outer', 'core', 'rep'), 0, 0, tiled=True)  26.1 us
    all_gather x1, waiting for transfers between devices, body(): gathered = lax.all_gather(tiles, ('outer', 'rep'), axis=0, tiled=True)  15 us
    pallas_call x1, Pallas kernels, body(): pl.pallas_call(functools.partial(apply_kernel, limit, count), out_shape=j...  12.1 us
  transfers between devices with their start and end apart: 1, of which 1 were waited for; matrix products, arithmetic and copies ran while one was open for 0% of the time, Pallas kernels for 1%

profile of v1, /device:TPU:1, one launch (start us, length us, event | category | flops | bytes accessed | tf_op | source)
XLA Modules:
  0.0 118.9 jit_solution(11892892134008823933)
XLA Ops:
  6.5 0.0 all-gather.2.cloned.1.call-start
  6.5 2.0 %pick.1 = (bf16[4,128,128]{2,1,0:T(8,128)(2,1)}, f32[32,8,128]{2,1,0:T(8,128)}) custom-call(s32[1,7]{1,0:T(1,128)} %mask_ref.1, f32[1,7,128,128]{3,2,1,0:T(8,128)} %master_ref.1, bf16[1,7,128,128]{3,2,1,0:T(8,128)(2,1)} %synced_ref.1), custom_call_target="tpu_custom_call" | custom-call | tf_op jit(solution)/shard_map/pick/pallas_call | solution.py:73
  8.5 0.0 all-gather.2.cloned.1.call-update
  8.5 26.1 %all_to_all.10.notes_ref = f32[32,8,128]{2,1,0:T(8,128)} all-to-all(f32[32,8,128]{2,1,0:T(8,128)} %get-tuple-element.9), channel_id=1, replica_groups=mesh['outer'=4,'z'=32,'core'=2,'rep'=4] {'outer','core','rep'}, dimensions={0} | all-to-all | bytes 262144 | tf_op jit(solution)/shard_map/plane_sum/all_to_all | solution.py:85
  34.6 1.7 %plane_sum.1 = (f32[32,8,128]{2,1,0:T(8,128)}, s32[16,128]{1,0:T(8,128)}) custom-call(f32[32,8,128]{2,1,0:T(8,128)} %all_to_all.10.notes_ref), custom_call_target="tpu_custom_call" | custom-call | tf_op jit(solution)/shard_map/plane_sum/pallas_call | solution.py:86
  36.3 48.6 %all_to_all.11.sums_ref = f32[32,8,128]{2,1,0:T(8,128)} all-to-all(f32[32,8,128]{2,1,0:T(8,128)} %get-tuple-element.11), channel_id=1, replica_groups=mesh['outer'=4,'z'=32,'core'=2,'rep'=4] {'z'}, dimensions={0} | all-to-all | bytes 262144 | tf_op jit(solution)/shard_map/z_sum/all_to_all | solution.py:96
  84.9 15.0 %all-gather.2.cloned.1.call-done.tiles_ref = bf16[64,128,128]{2,1,0:T(8,128)(2,1)} async-done(((bf16[4,128,128]{2,1,0:T(8,128)(2,1)}), bf16[64,128,128]{2,1,0:T(8,128)(2,1)}) %all-gather.2.cloned.1.call-update) | async-done | bytes 2097168 | tf_op jit(solution)/shard_map/gather/all_gather | solution.py:83
  99.9 12.1 %apply.1 = bf16[2,128,7168]{2,1,0:T(8,128)(2,1)} custom-call(s32[16,128]{1,0:T(8,128)} %get-tuple-element.10.table_ref, f32[32,8,128]{2,1,0:T(8,128)} %all_to_all.11.sums_ref, bf16[64,128,128]{2,1,0:T(8,128)(2,1)} %all-gather.2.cloned.1.call-done.tiles_ref, bf16[2,128,7168]{2,1,0:T(8,128)(2,1)} %resident_ref.1), custom_call_target="tpu_custom_call" | custom-call | tf_op jit(solution)/shard_map/apply/pallas_call | solution.py:101
Async XLA Ops:
  6.5 93.3 %all-gather.2.cloned.1.call-start = ((), (), s32[]{:S(2)}) async-start(), calls=%async_computation.2 | async-start | bytes 2228224 | tf_op jit(solution)/shard_map/gather/all_gather | solution.py:83
Sparse Core Ops, SparseCore 0:
  11.5 88.2 all-gather.1

commit v2 on v1

v2 whole, which is shorter than its diff:
```python
import functools
import math

import jax
import jax.numpy as jnp
from jax import lax
from jax.experimental import pallas as pl
from jax.experimental.pallas import tpu as pltpu
from jax.sharding import Mesh, PartitionSpec as P

SLOTS = 4
TILE = 128
PARTS = 8
ROOM = 12 * 2**20
ALL = ("outer", "z", "core", "rep")
PLANE = ("outer", "core", "rep")


def pick_kernel(mask_ref, master_ref, synced_ref, tiles_ref, note_ref):
    count = mask_ref.shape[1]
    where = [jnp.int32(0)] * SLOTS
    used = jnp.int32(0)
    for i in range(count):
        listed = mask_ref[0, i] > 0
        for s in range(SLOTS):
            where[s] = jnp.where(listed & (used == s), i, where[s])
        used = used + listed.astype(jnp.int32)
    squares = jnp.zeros((8, TILE), jnp.float32)
    for s in range(SLOTS):
        delta = (master_ref[0, where[s]] - synced_ref[0, where[s]].astype(jnp.float32)).astype(jnp.bfloat16)
        tiles_ref[s] = delta
        wide = jnp.where(used > s, delta.astype(jnp.float32), 0.0)
        squares = squares + jnp.sum((wide * wide).reshape(-1, 8, TILE), axis=0)
    lane = lax.broadcasted_iota(jnp.int32, note_ref.shape[1:], 1)
    note = jnp.where(lane == 0, jnp.sum(squares), 0.0)
    for k, entry in enumerate([used] + where):
        note = jnp.where(lane == 1 + k, entry.astype(jnp.float32), note)
    note_ref[...] = jnp.broadcast_to(note[None], note_ref.shape)


def plane_kernel(outers, reps, notes_ref, sum_ref, table_ref):
    core = lax.axis_index("core")
    total = jnp.sum(notes_ref[...], axis=0)
    sum_ref[...] = jnp.broadcast_to(total[:, 0:1], total.shape)
    lane = lax.broadcasted_iota(jnp.int32, (reps, TILE), 1)
    for y in range(outers):
        mine = notes_ref[pl.ds((y * 2 + core) * reps, reps), 0, :]
        table_ref[y * reps:(y + 1) * reps, :] = jnp.where(lane == 0, 0.0, mine).astype(jnp.int32)


def each_listed(table_ref, act):
    shards = table_ref.shape[0]
    tile_count = 7

    def over_shards(j, _):
        def over_slots(s, _):
            act(j * SLOTS + s, j * tile_count + table_ref[j, 2 + s])
            return 0

        return lax.fori_loop(0, table_ref[j, 1], over_slots, 0)

    lax.fori_loop(0, shards, over_shards, 0)


def tile_of(ref, tile):
    layers, rows, width = ref.shape
    per_layer = width // TILE
    layer = tile // per_layer
    start = pl.multiple_of((tile - layer * per_layer) * TILE, TILE)
    return ref.at[layer, :, pl.ds(start, TILE)]


def base_kernel(table_ref, resident_ref, base_ref, stage_ref, whole_sem, tile_sem):
    layers, rows, _ = resident_ref.shape
    chunk = rows // PARTS
    copies = [
        pltpu.make_async_copy(
            resident_ref.at[l, pl.ds(k * chunk, chunk)], base_ref.at[l, pl.ds(k * chunk, chunk)], whole_sem.at[l, k]
        )
        for l in range(layers)
        for k in range(PARTS)
    ]

    def staged(slot, tile):
        return pltpu.make_async_copy(tile_of(resident_ref, tile), stage_ref.at[slot], tile_sem.at[slot])

    each_listed(table_ref, lambda slot, tile: staged(slot, tile).start())
    for copy in copies:
        copy.start()
    each_listed(table_ref, lambda slot, tile: staged(slot, tile).wait())
    for copy in copies:
        copy.wait()


def apply_kernel(limit, table_ref, sums_ref, stage_ref, tiles_ref, base_ref, out_ref, new_ref, sem):
    del base_ref
    total = jnp.sum(sums_ref[...], axis=0)
    factor = jnp.minimum(jnp.float32(1.0), limit / jnp.sqrt(total))

    def written(slot, tile):
        return pltpu.make_async_copy(new_ref.at[slot], tile_of(out_ref, tile), sem.at[slot])

    def update(slot, tile):
        moved = factor[None] * tiles_ref[slot].astype(jnp.float32).reshape(-1, 8, TILE)
        new_ref[slot] = (stage_ref[slot].astype(jnp.float32) + moved.reshape(TILE, TILE)).astype(jnp.bfloat16)
        written(slot, tile).start()

    each_listed(table_ref, update)
    each_listed(table_ref, lambda slot, tile: written(slot, tile).wait())


def body(master, synced, keep_mask, resident):
    outers, chips, cores, reps = (lax.axis_size(a) for a in ALL)
    _, count, side, _ = master.shape
    shards = outers * reps
    plane = shards * cores
    vmem = pl.BlockSpec(memory_space=pltpu.VMEM)
    smem = pl.BlockSpec(memory_space=pltpu.SMEM)
    hbm = pl.BlockSpec(memory_space=pltpu.HBM)
    params = pltpu.CompilerParams(vmem_limit_bytes=ROOM)
    with jax.named_scope("pick"):
        tiles, notes = pl.pallas_call(
            pick_kernel,
            out_shape=(
                jax.ShapeDtypeStruct((SLOTS, side, side), jnp.bfloat16),
                jax.ShapeDtypeStruct((plane, 8, TILE), jnp.float32),
            ),
            in_specs=[smem, vmem, vmem],
            out_specs=(vmem, vmem),
            compiler_params=params,
        )(keep_mask, master, synced)
    with jax.named_scope("plane_sum"):
        notes = lax.all_to_all(notes, PLANE, 0, 0, tiled=True)
        plane_total, table = pl.pallas_call(
            functools.partial(plane_kernel, outers, reps),
            out_shape=(
                jax.ShapeDtypeStruct((8, TILE), jnp.float32),
                jax.ShapeDtypeStruct((shards, TILE), jnp.int32),
            ),
            in_specs=[vmem],
            out_specs=(vmem, vmem),
            compiler_params=params,
        )(notes)
    tiles, plane_total = lax.optimization_barrier((tiles, plane_total))
    with jax.named_scope("gather"):
        spread = jnp.broadcast_to(tiles[None], (shards,) + tiles.shape)
        gathered = lax.all_to_all(spread, ("outer", "rep"), 0, 0, tiled=True)
        gathered = gathered.reshape(shards * SLOTS, side, side)
    with jax.named_scope("z_shift"):
        pairs = []
        for o in range(outers):
            for z in range(chips):
                for c in range(cores):
                    for r in range(reps):
                        there = (z + (o * cores + c) * reps + r - plane // 2 + 1) % chips
                        pairs.append(
                            (((o * chips + z) * cores + c) * reps + r, ((o * chips + there) * cores + c) * reps + r)
                        )
        other = lax.ppermute(plane_total, ALL, pairs)
    with jax.named_scope("base"):
        base, stage = pl.pallas_call(
            base_kernel,
            out_shape=(
                jax.ShapeDtypeStruct(resident.shape, resident.dtype),
                jax.ShapeDtypeStruct((shards * SLOTS, side, side), resident.dtype),
            ),
            in_specs=[smem, hbm],
            out_specs=(hbm, vmem),
            scratch_shapes=[
                pltpu.SemaphoreType.DMA((resident.shape[0], PARTS)),
                pltpu.SemaphoreType.DMA((shards * SLOTS,)),
            ],
            compiler_params=params,
            cost_estimate=pl.CostEstimate(flops=0, bytes_accessed=4 * resident.size, transcendentals=0),
        )(table, resident)
    other, gathered, base = lax.optimization_barrier((other, gathered, base))
    with jax.named_scope("z_sum"):
        sums = lax.all_to_all(jnp.broadcast_to(other[None], (plane, 8, TILE)), PLANE, 0, 0, tiled=True)
    limit = 0.25 * side * math.sqrt(count * plane * chips)
    limit = limit * math.sqrt(plane / chips)
    with jax.named_scope("apply"):
        return pl.pallas_call(
            functools.partial(apply_kernel, limit),
            out_shape=jax.ShapeDtypeStruct(resident.shape, resident.dtype),
            in_specs=[smem, vmem, vmem, vmem, hbm],
            out_specs=hbm,
            scratch_shapes=[
                pltpu.VMEM((shards * SLOTS, side, side), jnp.bfloat16),
                pltpu.SemaphoreType.DMA((shards * SLOTS,)),
            ],
            input_output_aliases={4: 0},
            compiler_params=params,
        )(table, sums, stage, gathered, base)


def solution(mesh):
    outers, tensors, reps = mesh.devices.shape
    fine = Mesh(mesh.devices.reshape(outers, tensors // 2, 2, reps), ALL)
    head = ("z", "core")
    placed = (
        P(head, ("outer", "rep"), None, None),
        P(head, ("outer", "rep"), None, None),
        P(head, ("outer", "rep")),
        P(None, head, None),
    )
    return jax.shard_map(
        body, mesh=fine, in_specs=placed, out_specs=P(None, head, None), check_vma=False
    )
```

time: 119 us -> 83.6 us (0.70)
  blocking collectives: 74.7 us -> 36.7 us
  starting transfers between devices: 0.01 us -> 20.5 us
  between operations: 13.4 us -> 0.06 us
  local copies, waits for them, and re-layouts: 0 us -> 9.39 us
  Pallas kernels: 15.8 us -> 7.67 us
  waiting for transfers between devices: 15 us -> 8.92 us
    all_to_all x2, blocking collectives: 74.7 us -> 36.7 us  [the longest x1 24.5 us: body(): notes = lax.all_to_all(notes, PLANE, 0, 0, tiled=True)]
    ppermute x0 -> x1, starting transfers between devices: none -> 16.8 us  [body(): other = lax.ppermute(plane_total, ALL, pairs)]
    all_gather x1 -> x0, waiting for transfers between devices: 15 us -> none  [body(): gathered = lax.all_gather(tiles, ('outer', 'rep'), axis=0, tiled=True)]
    all_to_all x0 -> x1, waiting for transfers between devices: none -> 8.92 us  [body(): gathered = lax.all_to_all(spread, ('outer', 'rep'), 0, 0, tiled=True)]
    unnamed x0 -> x12, local copies, waits for them, and re-layouts: none -> 7.56 us
    pallas_call x1 -> x2, Pallas kernels: 12.1 us -> 6.82 us  [the longest x1 4.22 us: body(): pl.pallas_call(base_kernel, out_shape=(jax.ShapeDtypeStruct(resident.shap...]
    all_to_all x0 -> x1, starting transfers between devices: none -> 3.72 us  [body(): gathered = lax.all_to_all(spread, ('outer', 'rep'), 0, 0, tiled=True)]
    broadcast_in_dim x0 -> x2, local copies, waits for them, and re-layouts: none -> 1.84 us  [the longest x1 1.83 us: body(): spread = jnp.broadcast_to(tiles[None], (shards,) + tiles.shape)]
  transfers between devices with their start and end apart: 1 -> 2, of which waited for: 1 -> 1; matrix products, arithmetic and copies ran while one was open for 0% -> 0% of each run, Pallas kernels for 1% -> 5%
where the time goes in v2:
time: 83.6 us; the launch traced here: 83.2 us
  blocking collectives  36.7 us (44%)
  starting transfers between devices  20.5 us (25%)
  local copies, waits for them, and re-layouts  9.39 us (11%)
  waiting for transfers between devices  8.92 us (11%)
  Pallas kernels  7.67 us (9%)
    all_to_all x1, blocking collectives, body(): notes = lax.all_to_all(notes, PLANE, 0, 0, tiled=True)  24.5 us
    ppermute x1, starting transfers between devices, body(): other = lax.ppermute(plane_total, ALL, pairs)  16.8 us
    all_to_all x1, blocking collectives, body(): lax.all_to_all(jnp.broadcast_to(other[None], (plane, 8, TILE)), PLANE, 0,...  12.2 us
    all_to_all x1, waiting for transfers between devices, body(): gathered = lax.all_to_all(spread, ('outer', 'rep'), 0, 0, tiled=True)  8.92 us
    unnamed x12, local copies, waits for them, and re-layouts  7.56 us
    pallas_call x1, Pallas kernels, body(): pl.pallas_call(base_kernel, out_shape=(jax.ShapeDtypeStruct(resident.shap...  4.22 us
    all_to_all x1, starting transfers between devices, body(): gathered = lax.all_to_all(spread, ('outer', 'rep'), 0, 0, tiled=True)  3.72 us
    pallas_call x1, Pallas kernels, body(): pl.pallas_call(functools.partial(apply_kernel, limit), out_shape=jax.Shap...  2.6 us
  transfers between devices with their start and end apart: 2, of which 1 were waited for; matrix products, arithmetic and copies ran while one was open for 0% of the time, Pallas kernels for 5%

profile of v2, /device:TPU:1, one launch (start us, length us, event | category | flops | bytes accessed | tf_op | source)
XLA Modules:
  0.0 83.2 jit_solution(15917569889546355874)
XLA Ops:
  0.0 0.0 copy-start.3
  0.0 1.0 %copy-done.3 = f32[1,7,128,128]{3,2,1,0:T(8,128)S(1)} copy-done((f32[1,7,128,128]{3,2,1,0:T(8,128)S(1)}, f32[1,7,128,128]{3,2,1,0:T(8,128)}, u32[]{:S(2)}) %copy-start.3) | copy-done | bytes 458776
  1.0 0.0 copy-start.4
  1.0 0.9 %copy-done.4 = bf16[1,7,128,128]{3,2,1,0:T(8,128)(2,1)S(1)} copy-done((bf16[1,7,128,128]{3,2,1,0:T(8,128)(2,1)S(1)}, bf16[1,7,128,128]{3,2,1,0:T(8,128)(2,1)}, u32[]{:S(2)}) %copy-start.4) | copy-done | bytes 229400
  2.0 0.0 copy-start.5
  2.0 0.7 copy-done.5
  2.6 0.8 pick.1
  3.4 24.5 %all_to_all.15.notes_ref = f32[32,8,128]{2,1,0:T(8,128)S(1)} all-to-all(f32[32,8,128]{2,1,0:T(8,128)S(1)} %get-tuple-element.16), channel_id=1, replica_groups=mesh['outer'=4,'z'=32,'core'=2,'rep'=4] {'outer','core','rep'}, dimensions={0} | all-to-all | bytes 262144 | tf_op jit(solution)/shard_map/plane_sum/all_to_all | solution.py:133
  27.9 0.1 plane_sum.1
  28.0 1.8 %broadcast_in_dim.4 = bf16[16,4,128,128]{3,2,1,0:T(8,128)(2,1)} broadcast(bf16[4,128,128]{2,1,0:T(8,128)(2,1)S(1)} %get-tuple-element.21), dimensions={1,2,3} | broadcast | bytes 2228224 | tf_op jit(solution)/shard_map/gather/broadcast_in_dim | solution.py:146
  29.8 3.7 %all-to-all-start.1 = ((bf16[16,4,128,128]{3,2,1,0:T(8,128)(2,1)}), bf16[16,4,128,128]{3,2,1,0:T(8,128)(2,1)S(1)}, u32[]{:S(2)}, u32[]{:S(2)}) async-start(bf16[16,4,128,128]{3,2,1,0:T(8,128)(2,1)} %broadcast_in_dim.4), calls=%async_computation.1 | async-start | bytes 4194304 | tf_op jit(solution)/shard_map/gather/all_to_all | solution.py:147
  33.5 16.8 %collective-permute-start = (f32[8,128]{1,0:T(8,128)S(1)}, f32[8,128]{1,0:T(8,128)S(1)}, u32[]{:S(2)}, u32[]{:S(2)}) collective-permute-start(f32[8,128]{1,0:T(8,128)S(1)} %get-tuple-element.20), channel_id=1, source_target_pairs={{0,136},{1,145},{2,154},{3,163},{4,172},{5,181},{6,190},{7,199},{8... | collective-permute-start | bytes 12296 | tf_op jit(solution)/shard_map/z_shift/ppermute | solution.py:159
  50.3 0.0 copy-start
  50.3 2.0 %copy-done = bf16[2,128,7168]{2,1,0:T(8,128)(2,1)S(1)} copy-done((bf16[2,128,7168]{2,1,0:T(8,128)(2,1)S(1)}, bf16[2,128,7168]{2,1,0:T(8,128)(2,1)}, u32[]{:S(2)}) %copy-start) | copy-done | bytes 3670040
  52.4 4.2 %base.1 = (bf16[2,128,7168]{2,1,0:T(8,128)(2,1)}, bf16[64,128,128]{2,1,0:T(8,128)(2,1)S(1)}) custom-call(s32[16,128]{1,0:T(8,128)S(1)} %get-tuple-element.17.table_ref, bf16[2,128,7168]{2,1,0:T(8,128)(2,1)S(1)} %copy-done), custom_call_target="tpu_custom_call" | custom-call | bytes 7340032 | tf_op jit(solution)/shard_map/base/pallas_call | solution.py:161
  56.6 0.0 copy-start.1
  56.6 1.3 %copy-done.1 = bf16[64,128,128]{2,1,0:T(8,128)(2,1)} copy-done((bf16[64,128,128]{2,1,0:T(8,128)(2,1)}, bf16[64,128,128]{2,1,0:T(8,128)(2,1)S(1)}, u32[]{:S(2)}) %copy-start.1) | copy-done | bytes 2097176
  57.9 0.0 collective-permute-done
  57.9 8.9 %all-to-all-done.1 = bf16[16,4,128,128]{3,2,1,0:T(8,128)(2,1)S(1)} async-done(((bf16[16,4,128,128]{3,2,1,0:T(8,128)(2,1)}), bf16[16,4,128,128]{3,2,1,0:T(8,128)(2,1)S(1)}, u32[]{:S(2)}, u32[]{:S(2)}) %all-to-all-start.1) | async-done | bytes 2097184 | tf_op jit(solution)/shard_map/gather/all_to_all | solution.py:147
  66.8 12.2 %all_to_all.16.sums_ref = f32[32,8,128]{2,1,0:T(8,128)S(1)} all-to-all(f32[32,8,128]{2,1,0:T(8,128)S(1)} %broadcast_in_dim.5), channel_id=1, replica_groups=mesh['outer'=4,'z'=32,'core'=2,'rep'=4] {'outer','core','rep'}, dimensions={0} | all-to-all | bytes 262144 | tf_op jit(solution)/shard_map/z_sum/all_to_all | solution.py:178
  79.0 0.0 copy-start.2
  79.0 1.6 %copy-done.2 = bf16[64,128,128]{2,1,0:T(8,128)(2,1)S(1)} copy-done((bf16[64,128,128]{2,1,0:T(8,128)(2,1)S(1)}, bf16[64,128,128]{2,1,0:T(8,128)(2,1)}, u32[]{:S(2)}) %copy-start.2) | copy-done | bytes 2097176
  80.6 2.6 %apply.1 = bf16[2,128,7168]{2,1,0:T(8,128)(2,1)} custom-call(s32[16,128]{1,0:T(8,128)S(1)} %get-tuple-element.17.table_ref, f32[32,8,128]{2,1,0:T(8,128)S(1)} %all_to_all.16.sums_ref, bf16[64,128,128]{2,1,0:T(8,128)(2,1)S(1)} %copy-done.2, bf16[64,128,128]{2,1,0:T(8,128)(2,1)S(1)} %bitcast.1, ...), custom_call_target="tpu_custom_call", output_to_operand_aliasing={{}: (4, {})} | custom-call | tf_op jit(solution)/shard_map/apply/pallas_call | solution.py:182
  (1 shorter events, 0.0 us)
Async XLA Ops:
  0.0 1.0 %copy-start.3 = (f32[1,7,128,128]{3,2,1,0:T(8,128)S(1)}, f32[1,7,128,128]{3,2,1,0:T(8,128)}, u32[]{:S(2)}) copy-start(f32[1,7,128,128]{3,2,1,0:T(8,128)} %master_ref.1) | copy-start | bytes 1376260
  1.0 0.9 %copy-start.4 = (bf16[1,7,128,128]{3,2,1,0:T(8,128)(2,1)S(1)}, bf16[1,7,128,128]{3,2,1,0:T(8,128)(2,1)}, u32[]{:S(2)}) copy-start(bf16[1,7,128,128]{3,2,1,0:T(8,128)(2,1)} %synced_ref.1) | copy-start | bytes 688132
  2.0 0.7 copy-start.5
  29.8 37.0 %all-to-all-start.1 = ((bf16[16,4,128,128]{3,2,1,0:T(8,128)(2,1)}), bf16[16,4,128,128]{3,2,1,0:T(8,128)(2,1)S(1)}, u32[]{:S(2)}, u32[]{:S(2)}) async-start(bf16[16,4,128,128]{3,2,1,0:T(8,128)(2,1)} %broadcast_in_dim.4), calls=%async_computation.1 | async-start | bytes 4194304 | tf_op jit(solution)/shard_map/gather/all_to_all | solution.py:147
  33.5 24.4 %collective-permute-start = (f32[8,128]{1,0:T(8,128)S(1)}, f32[8,128]{1,0:T(8,128)S(1)}, u32[]{:S(2)}, u32[]{:S(2)}) collective-permute-start(f32[8,128]{1,0:T(8,128)S(1)} %get-tuple-element.20), channel_id=1, source_target_pairs={{0,136},{1,145},{2,154},{3,163},{4,172},{5,181},{6,190},{7,199},{8... | collective-permute-start | bytes 12296 | tf_op jit(solution)/shard_map/z_shift/ppermute | solution.py:159
  50.3 2.0 %copy-start = (bf16[2,128,7168]{2,1,0:T(8,128)(2,1)S(1)}, bf16[2,128,7168]{2,1,0:T(8,128)(2,1)}, u32[]{:S(2)}) copy-start(bf16[2,128,7168]{2,1,0:T(8,128)(2,1)} %resident_ref.1) | copy-start | bytes 11010052
  56.6 1.3 %copy-start.1 = (bf16[64,128,128]{2,1,0:T(8,128)(2,1)}, bf16[64,128,128]{2,1,0:T(8,128)(2,1)S(1)}, u32[]{:S(2)}) copy-start(bf16[64,128,128]{2,1,0:T(8,128)(2,1)S(1)} %get-tuple-element.24.stage_ref) | copy-start | bytes 6291460
  79.0 1.6 %copy-start.2 = (bf16[64,128,128]{2,1,0:T(8,128)(2,1)S(1)}, bf16[64,128,128]{2,1,0:T(8,128)(2,1)}, u32[]{:S(2)}) copy-start(bf16[64,128,128]{2,1,0:T(8,128)(2,1)} %copy-done.1) | copy-start | bytes 6291460

commit v3 on v1

v3 whole, which is shorter than its diff:
```python
import functools
import math

import jax
import jax.numpy as jnp
from jax import lax
from jax.experimental import pallas as pl
from jax.experimental.pallas import tpu as pltpu
from jax.sharding import Mesh, PartitionSpec as P

SLOTS = 4
TILE = 128
SMALL = 4 * 2**20
LARGE = 53 * 10**6
ALL = ("outer", "z", "core", "rep")
PLANE = ("outer", "core", "rep")
PEERS = ("outer", "rep")


def pick_kernel(mask_hbm, master_hbm, synced_hbm, spread_hbm, note_ref, mask_ref, master_ref, synced_ref, tiles_ref, sem, out_sem):
    loads = [
        pltpu.make_async_copy(mask_hbm, mask_ref, sem.at[0]),
        pltpu.make_async_copy(master_hbm, master_ref, sem.at[1]),
        pltpu.make_async_copy(synced_hbm, synced_ref, sem.at[2]),
    ]
    for load in loads:
        load.start()
    loads[0].wait()
    where = [jnp.int32(0)] * SLOTS
    used = jnp.int32(0)
    for i in range(mask_ref.shape[1]):
        listed = mask_ref[0, i] > 0
        for s in range(SLOTS):
            where[s] = jnp.where(listed & (used == s), i, where[s])
        used = used + listed.astype(jnp.int32)
    for load in loads[1:]:
        load.wait()
    squares = jnp.zeros((8, TILE), jnp.float32)
    for s in range(SLOTS):
        delta = (master_ref[0, where[s]] - synced_ref[0, where[s]].astype(jnp.float32)).astype(jnp.bfloat16)
        tiles_ref[s] = delta
        wide = jnp.where(used > s, delta.astype(jnp.float32), 0.0)
        squares = squares + jnp.sum((wide * wide).reshape(-1, 8, TILE), axis=0)
    sends = [
        pltpu.make_async_copy(tiles_ref, spread_hbm.at[j], out_sem.at[j]) for j in range(spread_hbm.shape[0])
    ]
    for send in sends:
        send.start()
    lane = lax.broadcasted_iota(jnp.int32, note_ref.shape, 1)
    note = jnp.where(lane == 0, jnp.sum(squares), 0.0)
    for k, entry in enumerate([used] + where):
        note = jnp.where(lane == 1 + k, entry.astype(jnp.float32), note)
    note_ref[...] = note
    for send in sends:
        send.wait()


def column_kernel(column_ref, note_ref, notes_ref):
    total = jnp.sum(column_ref[...], axis=0, keepdims=True)
    note = note_ref[...]
    lane = lax.broadcasted_iota(jnp.int32, note.shape, 1)
    note = jnp.where(lane == 0, total, note)
    notes_ref[...] = jnp.broadcast_to(note[None], notes_ref.shape)


def plane_kernel(limit, outers, reps, notes_ref, factor_ref, table_ref):
    core = lax.axis_index("core")
    total = jnp.sum(notes_ref[...], axis=0)
    total = jnp.broadcast_to(total[:, 0:1], total.shape)
    factor_ref[...] = jnp.minimum(jnp.float32(1.0), limit / jnp.sqrt(total))
    lane = lax.broadcasted_iota(jnp.int32, (reps, TILE), 1)
    for y in range(outers):
        mine = notes_ref[pl.ds((y * 2 + core) * reps, reps), 0, :]
        table_ref[y * reps:(y + 1) * reps, :] = jnp.where(lane == 0, 0.0, mine).astype(jnp.int32)


def apply_kernel(count, table_ref, factor_ref, tiles_ref, resident_hbm, out_hbm, rows_ref, in_sem, out_sem):
    shards = table_ref.shape[0]
    wide = count * TILE
    per_layer = resident_hbm.shape[2] // wide

    def block(ref, j):
        return ref.at[j // per_layer, :, pl.ds((j % per_layer) * wide, wide)]

    loads = [pltpu.make_async_copy(block(resident_hbm, j), block(rows_ref, j), in_sem.at[j]) for j in range(shards)]
    stores = [pltpu.make_async_copy(block(rows_ref, j), block(out_hbm, j), out_sem.at[j]) for j in range(shards)]
    for load in loads:
        load.start()
    factor = factor_ref[...][None]
    for j in range(shards):
        loads[j].wait()

        def update(s, _):
            start = pl.multiple_of((j % per_layer) * wide + table_ref[j, 2 + s] * TILE, TILE)
            place = (j // per_layer, slice(None), pl.ds(start, TILE))
            moved = (factor * tiles_ref[j * SLOTS + s].astype(jnp.float32).reshape(-1, 8, TILE)).reshape(TILE, TILE)
            rows_ref[place] = (rows_ref[place].astype(jnp.float32) + moved).astype(jnp.bfloat16)
            return 0

        lax.fori_loop(0, table_ref[j, 1], update, 0)
        stores[j].start()
    for store in stores:
        store.wait()


def body(master, synced, keep_mask, resident):
    outers, chips, cores, reps = (lax.axis_size(a) for a in ALL)
    _, count, side, _ = master.shape
    shards = outers * reps
    plane = shards * cores
    limit = 0.25 * side * math.sqrt(count * plane * chips)
    vmem = pl.BlockSpec(memory_space=pltpu.VMEM)
    smem = pl.BlockSpec(memory_space=pltpu.SMEM)
    hbm = pl.BlockSpec(memory_space=pl.ANY)
    small = pltpu.CompilerParams(vmem_limit_bytes=SMALL)
    large = pltpu.CompilerParams(vmem_limit_bytes=LARGE)
    with jax.named_scope("pick"):
        spread, note = pl.pallas_call(
            pick_kernel,
            out_shape=(
                jax.ShapeDtypeStruct((shards, SLOTS, side, side), jnp.bfloat16),
                jax.ShapeDtypeStruct((8, TILE), jnp.float32),
            ),
            in_specs=[hbm, hbm, hbm],
            out_specs=(hbm, vmem),
            scratch_shapes=[
                pltpu.SMEM(keep_mask.shape, keep_mask.dtype),
                pltpu.VMEM(master.shape, master.dtype),
                pltpu.VMEM(synced.shape, synced.dtype),
                pltpu.VMEM((SLOTS, side, side), jnp.bfloat16),
                pltpu.SemaphoreType.DMA((3,)),
                pltpu.SemaphoreType.DMA((shards,)),
            ],
        )(keep_mask, master, synced)
    with jax.named_scope("gather"):
        gathered = lax.all_to_all(spread, PEERS, 0, 0, tiled=True)
        gathered = gathered.reshape(shards * SLOTS, side, side)
    with jax.named_scope("z_sum"):
        column = lax.all_gather(note[:1], "z", axis=0, tiled=True)
        notes = pl.pallas_call(
            column_kernel,
            out_shape=jax.ShapeDtypeStruct((plane, 8, TILE), jnp.float32),
            in_specs=[vmem, vmem],
            out_specs=vmem,
            compiler_params=small,
        )(column, note)
    notes, gathered = lax.optimization_barrier((notes, gathered))
    with jax.named_scope("plane_sum"):
        notes = lax.all_to_all(notes, PLANE, 0, 0, tiled=True)
        factor, table = pl.pallas_call(
            functools.partial(plane_kernel, limit, outers, reps),
            out_shape=(
                jax.ShapeDtypeStruct((8, TILE), jnp.float32),
                jax.ShapeDtypeStruct((shards, TILE), jnp.int32),
            ),
            in_specs=[vmem],
            out_specs=(vmem, vmem),
            compiler_params=small,
        )(notes)
    with jax.named_scope("apply"):
        return pl.pallas_call(
            functools.partial(apply_kernel, count),
            out_shape=jax.ShapeDtypeStruct(resident.shape, resident.dtype),
            in_specs=[smem, vmem, vmem, hbm],
            out_specs=hbm,
            scratch_shapes=[
                pltpu.VMEM(resident.shape, resident.dtype),
                pltpu.SemaphoreType.DMA((shards,)),
                pltpu.SemaphoreType.DMA((shards,)),
            ],
            compiler_params=large,
        )(table, factor, gathered, resident)


def solution(mesh):
    outers, tensors, reps = mesh.devices.shape
    fine = Mesh(mesh.devices.reshape(outers, tensors // 2, 2, reps), ALL)
    head = ("z", "core")
    placed = (
        P(head, PEERS, None, None),
        P(head, PEERS, None, None),
        P(head, PEERS),
        P(None, head, None),
    )
    return jax.shard_map(
        body, mesh=fine, in_specs=placed, out_specs=P(None, head, None), check_vma=False
    )
```

time: 119 us -> 98.9 us (0.83)
  waiting for transfers between devices: 15 us -> 0.01 us
  between operations: 13.4 us -> 0.05 us
  blocking collectives: 74.7 us -> 83.2 us
  Pallas kernels: 15.8 us -> 7.75 us
  starting transfers between devices: 0.01 us -> 7.6 us
    all_gather x0 -> x1, blocking collectives: none -> 55.1 us  [body(): column = lax.all_gather(note[:1], 'z', axis=0, tiled=True)]
    all_to_all x2 -> x1, blocking collectives: 74.7 us -> 28.1 us  [body(): notes = lax.all_to_all(notes, PLANE, 0, 0, tiled=True)]
    all_gather x1 -> x0, waiting for transfers between devices: 15 us -> none  [body(): gathered = lax.all_gather(tiles, ('outer', 'rep'), axis=0, tiled=True)]
    pallas_call x3 -> x4, Pallas kernels: 15.8 us -> 7.75 us  [the longest x1 4.45 us: body(): pl.pallas_call(functools.partial(apply_kernel, count), out_shape=jax.Shap...]
    all_to_all x0 -> x1, starting transfers between devices: none -> 7.6 us  [body(): gathered = lax.all_to_all(spread, PEERS, 0, 0, tiled=True)]
  transfers between devices with their start and end apart: 1 -> 1, of which waited for: 1 -> 0; matrix products, arithmetic and copies ran while one was open for 0% -> 0% of each run, Pallas kernels for 1% -> 0%
where the time goes in v3:
time: 98.9 us; the launch traced here: 98.6 us
  blocking collectives  83.2 us (84%)
  Pallas kernels  7.75 us (8%)
  starting transfers between devices  7.6 us (8%)
    all_gather x1, blocking collectives, body(): column = lax.all_gather(note[:1], 'z', axis=0, tiled=True)  55.1 us
    all_to_all x1, blocking collectives, body(): notes = lax.all_to_all(notes, PLANE, 0, 0, tiled=True)  28.1 us
    all_to_all x1, starting transfers between devices, body(): gathered = lax.all_to_all(spread, PEERS, 0, 0, tiled=True)  7.6 us
    pallas_call x1, Pallas kernels, body(): pl.pallas_call(functools.partial(apply_kernel, count), out_shape=jax.Shap...  4.45 us
    pallas_call x1, Pallas kernels, body(): pl.pallas_call(pick_kernel, out_shape=(jax.ShapeDtypeStruct((shards, SLOT...  3.17 us
  transfers between devices with their start and end apart: 1, of which 0 were waited for; matrix products, arithmetic and copies ran while one was open for 0% of the time, Pallas kernels for 0%

profile of v3, /device:TPU:1, one launch (start us, length us, event | category | flops | bytes accessed | tf_op | source)
XLA Modules:
  0.0 98.6 jit_solution(1203448946698592419)
XLA Ops:
  0.0 3.2 %pick.1 = (bf16[16,4,128,128]{3,2,1,0:T(8,128)(2,1)}, f32[8,128]{1,0:T(8,128)}) custom-call(s32[1,7]{1,0:T(1,128)} %mask_hbm.1, f32[1,7,128,128]{3,2,1,0:T(8,128)} %master_hbm.1, bf16[1,7,128,128]{3,2,1,0:T(8,128)(2,1)} %synced_hbm.1), custom_call_target="tpu_custom_call" | custom-call | tf_op jit(solution)/shard_map/pick/pallas_call | solution.py:118
  3.2 0.0 copy-start
  3.2 7.6 %all-to-all-start = ((bf16[16,4,128,128]{3,2,1,0:T(8,128)(2,1)}), bf16[16,4,128,128]{3,2,1,0:T(8,128)(2,1)S(1)}, u32[]{:S(2)}, u32[]{:S(2)}) async-start(bf16[16,4,128,128]{3,2,1,0:T(8,128)(2,1)} %get-tuple-element.12), calls=%async_computation | async-start | bytes 4194304 | tf_op jit(solution)/shard_map/gather/all_to_all | solution.py:136
  10.8 0.0 copy-done
  10.8 55.1 %all-gather = f32[32,1,128]{2,1,0:T(1,128)S(1)} all-gather(f32[1,1,128]{2,1,0:T(1,128)S(1)} %slice_bitcast_fusion), channel_id=1, replica_groups=mesh['outer'=4,'z'=32,'core'=2,'rep'=4] {'z'}, dimensions={0}, use_global_device_ids=true | all-gather | bytes 16896 | tf_op jit(solution)/shard_map/z_sum/all_gather | solution.py:139
  66.0 0.0 all-to-all-done
  66.0 28.1 %all_to_all.10.notes_ref = f32[32,8,128]{2,1,0:T(8,128)S(1)} all-to-all(f32[32,8,128]{2,1,0:T(8,128)S(1)} %z_sum.1), channel_id=1, replica_groups=mesh['outer'=4,'z'=32,'core'=2,'rep'=4] {'outer','core','rep'}, dimensions={0} | all-to-all | bytes 262144 | tf_op jit(solution)/shard_map/plane_sum/all_to_all | solution.py:149
  94.0 0.1 plane_sum.1
  94.1 4.4 %apply.1 = bf16[2,128,7168]{2,1,0:T(8,128)(2,1)} custom-call(s32[16,128]{1,0:T(8,128)S(1)} %get-tuple-element.14.table_ref, f32[8,128]{1,0:T(8,128)S(1)} %get-tuple-element.15.factor_ref, bf16[64,128,128]{2,1,0:T(8,128)(2,1)S(1)} %bitcast.4, bf16[2,128,7168]{2,1,0:T(8,128)(2,1)} %resident_hbm.1), custom_call_target="tpu_custom_call" | custom-call | tf_op jit(solution)/shard_map/apply/pallas_call | solution.py:161
  (2 shorter events, 0.0 us)
Async XLA Ops:
  3.2 7.6 %copy-start = (f32[8,128]{1,0:T(8,128)S(1)}, f32[8,128]{1,0:T(8,128)}, u32[]{:S(2)}) copy-start(f32[8,128]{1,0:T(8,128)} %get-tuple-element.11.note_ref) | copy-start | bytes 12292
  3.2 62.8 %all-to-all-start = ((bf16[16,4,128,128]{3,2,1,0:T(8,128)(2,1)}), bf16[16,4,128,128]{3,2,1,0:T(8,128)(2,1)S(1)}, u32[]{:S(2)}, u32[]{:S(2)}) async-start(bf16[16,4,128,128]{3,2,1,0:T(8,128)(2,1)} %get-tuple-element.12), calls=%async_computation | async-start | bytes 4194304 | tf_op jit(solution)/shard_map/gather/all_to_all | solution.py:136

commit v4 on v2

v4 whole, which is shorter than its diff:
```python
import functools
import math

import jax
import jax.numpy as jnp
from jax import lax
from jax.experimental import pallas as pl
from jax.experimental.pallas import tpu as pltpu
from jax.sharding import Mesh, PartitionSpec as P

SLOTS = 4
TILE = 128
PARTS = 8
SMALL = 4 * 2**20
LARGE = 53 * 10**6
PICK = 568 * 10**5
ALL = ("outer", "z", "core", "rep")
PLANE = ("outer", "core", "rep")
PEERS = ("outer", "rep")


def pick_kernel(mask_hbm, master_hbm, synced_hbm, spread_hbm, notes_ref, mask_ref, master_ref, synced_ref, tiles_ref, sem, out_sem):
    loads = [
        pltpu.make_async_copy(mask_hbm, mask_ref, sem.at[0]),
        pltpu.make_async_copy(master_hbm, master_ref, sem.at[1]),
        pltpu.make_async_copy(synced_hbm, synced_ref, sem.at[2]),
    ]
    for load in loads:
        load.start()
    loads[0].wait()
    where = [jnp.int32(0)] * SLOTS
    used = jnp.int32(0)
    for i in range(mask_ref.shape[1]):
        listed = mask_ref[0, i] > 0
        for s in range(SLOTS):
            where[s] = jnp.where(listed & (used == s), i, where[s])
        used = used + listed.astype(jnp.int32)
    for load in loads[1:]:
        load.wait()
    squares = jnp.zeros((8, TILE), jnp.float32)
    for s in range(SLOTS):
        delta = (master_ref[0, where[s]] - synced_ref[0, where[s]].astype(jnp.float32)).astype(jnp.bfloat16)
        tiles_ref[s] = delta
        wide = jnp.where(used > s, delta.astype(jnp.float32), 0.0)
        squares = squares + jnp.sum((wide * wide).reshape(-1, 8, TILE), axis=0)
    sends = [
        pltpu.make_async_copy(tiles_ref, spread_hbm.at[j], out_sem.at[j]) for j in range(spread_hbm.shape[0])
    ]
    for send in sends:
        send.start()
    lane = lax.broadcasted_iota(jnp.int32, notes_ref.shape[1:], 1)
    note = jnp.where(lane == 0, jnp.sum(squares), 0.0)
    for k, entry in enumerate([used] + where):
        note = jnp.where(lane == 1 + k, entry.astype(jnp.float32), note)
    notes_ref[...] = jnp.broadcast_to(note[None], notes_ref.shape)
    for send in sends:
        send.wait()


def plane_kernel(outers, reps, notes_ref, sum_ref, table_ref):
    core = lax.axis_index("core")
    total = jnp.sum(notes_ref[...], axis=0)
    sum_ref[...] = jnp.broadcast_to(total[:, 0:1], total.shape)
    lane = lax.broadcasted_iota(jnp.int32, (reps, TILE), 1)
    for y in range(outers):
        mine = notes_ref[pl.ds((y * 2 + core) * reps, reps), 0, :]
        table_ref[y * reps:(y + 1) * reps, :] = jnp.where(lane == 0, 0.0, mine).astype(jnp.int32)


def each_listed(table_ref, act):
    shards = table_ref.shape[0]
    tile_count = 7

    def over_shards(j, _):
        def over_slots(s, _):
            act(j * SLOTS + s, j * tile_count + table_ref[j, 2 + s])
            return 0

        return lax.fori_loop(0, table_ref[j, 1], over_slots, 0)

    lax.fori_loop(0, shards, over_shards, 0)


def tile_of(ref, tile):
    layers, rows, width = ref.shape
    per_layer = width // TILE
    layer = tile // per_layer
    start = pl.multiple_of((tile - layer * per_layer) * TILE, TILE)
    return ref.at[layer, :, pl.ds(start, TILE)]


def base_kernel(resident_ref, base_ref, sem):
    layers, rows, _ = resident_ref.shape
    chunk = rows // PARTS
    copies = [
        pltpu.make_async_copy(
            resident_ref.at[l, pl.ds(k * chunk, chunk)], base_ref.at[l, pl.ds(k * chunk, chunk)], sem.at[l, k]
        )
        for l in range(layers)
        for k in range(PARTS)
    ]
    for copy in copies:
        copy.start()
    for copy in copies:
        copy.wait()


def apply_kernel(limit, table_ref, sums_ref, tiles_ref, resident_ref, base_ref, out_ref, new_ref, in_sem, out_sem):
    del base_ref

    def loaded(slot, tile):
        return pltpu.make_async_copy(tile_of(resident_ref, tile), new_ref.at[slot], in_sem.at[slot])

    def written(slot, tile):
        return pltpu.make_async_copy(new_ref.at[slot], tile_of(out_ref, tile), out_sem.at[slot])

    each_listed(table_ref, lambda slot, tile: loaded(slot, tile).start())
    total = jnp.sum(sums_ref[...], axis=0)
    factor = jnp.minimum(jnp.float32(1.0), limit / jnp.sqrt(total))

    def update(slot, tile):
        loaded(slot, tile).wait()
        moved = factor[None] * tiles_ref[slot].astype(jnp.float32).reshape(-1, 8, TILE)
        new_ref[slot] = (new_ref[slot].astype(jnp.float32) + moved.reshape(TILE, TILE)).astype(jnp.bfloat16)
        written(slot, tile).start()

    each_listed(table_ref, update)
    each_listed(table_ref, lambda slot, tile: written(slot, tile).wait())


def body(master, synced, keep_mask, resident):
    outers, chips, cores, reps = (lax.axis_size(a) for a in ALL)
    _, count, side, _ = master.shape
    shards = outers * reps
    plane = shards * cores
    vmem = pl.BlockSpec(memory_space=pltpu.VMEM)
    smem = pl.BlockSpec(memory_space=pltpu.SMEM)
    hbm = pl.BlockSpec(memory_space=pl.ANY)
    small = pltpu.CompilerParams(vmem_limit_bytes=SMALL)
    large = pltpu.CompilerParams(vmem_limit_bytes=LARGE)
    with jax.named_scope("pick"):
        spread, notes = pl.pallas_call(
            pick_kernel,
            out_shape=(
                jax.ShapeDtypeStruct((shards, SLOTS, side, side), jnp.bfloat16),
                jax.ShapeDtypeStruct((plane, 8, TILE), jnp.float32),
            ),
            in_specs=[hbm, hbm, hbm],
            out_specs=(hbm, vmem),
            scratch_shapes=[
                pltpu.SMEM(keep_mask.shape, keep_mask.dtype),
                pltpu.VMEM(master.shape, master.dtype),
                pltpu.VMEM(synced.shape, synced.dtype),
                pltpu.VMEM((SLOTS, side, side), jnp.bfloat16),
                pltpu.SemaphoreType.DMA((3,)),
                pltpu.SemaphoreType.DMA((shards,)),
            ],
            compiler_params=pltpu.CompilerParams(vmem_limit_bytes=PICK),
        )(keep_mask, master, synced)
    with jax.named_scope("plane_sum"):
        notes = lax.all_to_all(notes, PLANE, 0, 0, tiled=True)
        plane_total, table = pl.pallas_call(
            functools.partial(plane_kernel, outers, reps),
            out_shape=(
                jax.ShapeDtypeStruct((8, TILE), jnp.float32),
                jax.ShapeDtypeStruct((shards, TILE), jnp.int32),
            ),
            in_specs=[vmem],
            out_specs=(vmem, vmem),
            compiler_params=small,
        )(notes)
    spread, plane_total = lax.optimization_barrier((spread, plane_total))
    with jax.named_scope("gather"):
        gathered = lax.all_to_all(spread, PEERS, 0, 0, tiled=True)
        gathered = gathered.reshape(shards * SLOTS, side, side)
    with jax.named_scope("z_shift"):
        pairs = []
        for o in range(outers):
            for z in range(chips):
                for c in range(cores):
                    for r in range(reps):
                        there = (z + (o * cores + c) * reps + r - plane // 2 + 1) % chips
                        pairs.append(
                            (((o * chips + z) * cores + c) * reps + r, ((o * chips + there) * cores + c) * reps + r)
                        )
        other = lax.ppermute(plane_total, ALL, pairs)
    with jax.named_scope("base"):
        base = pl.pallas_call(
            base_kernel,
            out_shape=jax.ShapeDtypeStruct(resident.shape, resident.dtype),
            in_specs=[hbm],
            out_specs=hbm,
            scratch_shapes=[pltpu.SemaphoreType.DMA((resident.shape[0], PARTS))],
            compiler_params=large,
            cost_estimate=pl.CostEstimate(flops=0, bytes_accessed=4 * resident.size, transcendentals=0),
        )(resident)
    other, gathered, base = lax.optimization_barrier((other, gathered, base))
    with jax.named_scope("z_sum"):
        sums = lax.all_to_all(jnp.broadcast_to(other[None], (plane, 8, TILE)), PLANE, 0, 0, tiled=True)
    limit = 0.25 * side * math.sqrt(count * plane * chips)
    limit = limit * math.sqrt(plane / chips)
    with jax.named_scope("apply"):
        return pl.pallas_call(
            functools.partial(apply_kernel, limit),
            out_shape=jax.ShapeDtypeStruct(resident.shape, resident.dtype),
            in_specs=[smem, vmem, vmem, hbm, hbm],
            out_specs=hbm,
            scratch_shapes=[
                pltpu.VMEM((shards * SLOTS, side, side), jnp.bfloat16),
                pltpu.SemaphoreType.DMA((shards * SLOTS,)),
                pltpu.SemaphoreType.DMA((shards * SLOTS,)),
            ],
            input_output_aliases={4: 0},
            compiler_params=large,
        )(table, sums, gathered, resident, base)


def solution(mesh):
    outers, tensors, reps = mesh.devices.shape
    fine = Mesh(mesh.devices.reshape(outers, tensors // 2, 2, reps), ALL)
    head = ("z", "core")
    placed = (
        P(head, PEERS, None, None),
        P(head, PEERS, None, None),
        P(head, PEERS),
        P(None, head, None),
    )
    return jax.shard_map(
        body, mesh=fine, in_specs=placed, out_specs=P(None, head, None), check_vma=False
    )
```

time: 83.6 us -> 183 us (2.19)
  Pallas kernels: 7.67 us -> 120 us
  local copies, waits for them, and re-layouts: 9.39 us -> 0.01 us
  waiting for transfers between devices: 8.92 us -> 0.01 us
  blocking collectives: 36.7 us -> 42.7 us
    pallas_call x2, Pallas kernels: 4.97 us -> 116 us  [the longest x1 112 us: body(): pl.pallas_call(base_kernel, out_shape=jax.ShapeDtypeStruct(resident.shape...]
    all_to_all x1, waiting for transfers between devices: 8.92 us -> 0.01 us  [body(): gathered = lax.all_to_all(spread, PEERS, 0, 0, tiled=True)]
    unnamed x12 -> x0, local copies, waits for them, and re-layouts: 7.56 us -> none
    all_to_all x1, blocking collectives: 12.2 us -> 17.3 us  [body(): lax.all_to_all(jnp.broadcast_to(other[None], (plane, 8, TILE)), PLANE, 0,...]
  transfers between devices with their start and end apart: 2 -> 2, of which waited for: 1 -> 0; matrix products, arithmetic and copies ran while one was open for 0% -> 0% of each run, Pallas kernels for 5% -> 62%
where the time goes in v4:
time: 183 us
  Pallas kernels  120 us (66%)
  blocking collectives  42.7 us (23%)
  starting transfers between devices  19.8 us (11%)
    pallas_call x1, Pallas kernels, body(): pl.pallas_call(base_kernel, out_shape=jax.ShapeDtypeStruct(resident.shape...  112 us
    all_to_all x1, blocking collectives, body(): notes = lax.all_to_all(notes, PLANE, 0, 0, tiled=True)  25.4 us
    all_to_all x1, blocking collectives, body(): lax.all_to_all(jnp.broadcast_to(other[None], (plane, 8, TILE)), PLANE, 0,...  17.3 us
    ppermute x1, starting transfers between devices, body(): other = lax.ppermute(plane_total, ALL, pairs)  16.1 us
    pallas_call x1, Pallas kernels, body(): pl.pallas_call(functools.partial(apply_kernel, limit), out_shape=jax.Shap...  4.13 us
    all_to_all x1, starting transfers between devices, body(): gathered = lax.all_to_all(spread, PEERS, 0, 0, tiled=True)  3.72 us
  transfers between devices with their start and end apart: 2, of which 0 were waited for; matrix products, arithmetic and copies ran while one was open for 0% of the time, Pallas kernels for 62%

profile of v4, /device:TPU:1, one launch (start us, length us, event | category | flops | bytes accessed | tf_op | source)
XLA Modules:
  0.0 182.5 jit_solution(2525100974074849873)
XLA Ops:
  0.0 3.3 %pick.1 = (bf16[16,4,128,128]{3,2,1,0:T(8,128)(2,1)}, f32[32,8,128]{2,1,0:T(8,128)}) custom-call(s32[1,7]{1,0:T(1,128)} %mask_hbm.1, f32[1,7,128,128]{3,2,1,0:T(8,128)} %master_hbm.1, bf16[1,7,128,128]{3,2,1,0:T(8,128)(2,1)} %synced_hbm.1), custom_call_target="tpu_custom_call" | custom-call | tf_op jit(solution)/shard_map/pick/pallas_call | solution.py:142
  3.3 25.4 %all_to_all.15.notes_ref = f32[32,8,128]{2,1,0:T(8,128)S(1)} all-to-all(f32[32,8,128]{2,1,0:T(8,128)} %get-tuple-element.14), channel_id=1, replica_groups=mesh['outer'=4,'z'=32,'core'=2,'rep'=4] {'outer','core','rep'}, dimensions={0} | all-to-all | bytes 262144 | tf_op jit(solution)/shard_map/plane_sum/all_to_all | solution.py:161
  28.7 0.1 plane_sum.1
  28.8 3.7 %all-to-all-start.1 = ((bf16[16,4,128,128]{3,2,1,0:T(8,128)(2,1)}), bf16[16,4,128,128]{3,2,1,0:T(8,128)(2,1)S(1)}, u32[]{:S(2)}, u32[]{:S(2)}) async-start(bf16[16,4,128,128]{3,2,1,0:T(8,128)(2,1)} %get-tuple-element.19), calls=%async_computation.1 | async-start | bytes 4194304 | tf_op jit(solution)/shard_map/gather/all_to_all | solution.py:174
  32.5 16.1 %collective-permute-start = (f32[8,128]{1,0:T(8,128)S(1)}, f32[8,128]{1,0:T(8,128)S(1)}, u32[]{:S(2)}, u32[]{:S(2)}) collective-permute-start(f32[8,128]{1,0:T(8,128)S(1)} %get-tuple-element.18), channel_id=1, source_target_pairs={{0,136},{1,145},{2,154},{3,163},{4,172},{5,181},{6,190},{7,199},{8... | collective-permute-start | bytes 12296 | tf_op jit(solution)/shard_map/z_shift/ppermute | solution.py:186
  48.6 112.4 %base.1.base_ref = bf16[2,128,7168]{2,1,0:T(8,128)(2,1)} custom-call(bf16[2,128,7168]{2,1,0:T(8,128)(2,1)} %resident_ref.3), custom_call_target="tpu_custom_call" | custom-call | bytes 7340032 | tf_op jit(solution)/shard_map/base/pallas_call | solution.py:188
  161.0 0.0 collective-permute-done
  161.0 0.0 all-to-all-done.1
  161.1 17.3 %all_to_all.16.sums_ref = f32[32,8,128]{2,1,0:T(8,128)S(1)} all-to-all(f32[32,8,128]{2,1,0:T(8,128)S(1)} %broadcast_in_dim.2), channel_id=1, replica_groups=mesh['outer'=4,'z'=32,'core'=2,'rep'=4] {'outer','core','rep'}, dimensions={0} | all-to-all | bytes 262144 | tf_op jit(solution)/shard_map/z_sum/all_to_all | solution.py:199
  178.4 4.1 %apply.1 = bf16[2,128,7168]{2,1,0:T(8,128)(2,1)} custom-call(s32[16,128]{1,0:T(8,128)S(1)} %get-tuple-element.15.table_ref, f32[32,8,128]{2,1,0:T(8,128)S(1)} %all_to_all.16.sums_ref, bf16[64,128,128]{2,1,0:T(8,128)(2,1)S(1)} %bitcast.1, bf16[2,128,7168]{2,1,0:T(8,128)(2,1)} %resident_ref.3, ...), custom_call_target="tpu_custom_call", output_to_operand_aliasing={{}: (4, {})} | custom-call | tf_op jit(solution)/shard_map/apply/pallas_call | solution.py:203
  (1 shorter events, 0.0 us)
Async XLA Ops:
  28.8 132.3 %all-to-all-start.1 = ((bf16[16,4,128,128]{3,2,1,0:T(8,128)(2,1)}), bf16[16,4,128,128]{3,2,1,0:T(8,128)(2,1)S(1)}, u32[]{:S(2)}, u32[]{:S(2)}) async-start(bf16[16,4,128,128]{3,2,1,0:T(8,128)(2,1)} %get-tuple-element.19), calls=%async_computation.1 | async-start | bytes 4194304 | tf_op jit(solution)/shard_map/gather/all_to_all | solution.py:174
  32.5 128.5 %collective-permute-start = (f32[8,128]{1,0:T(8,128)S(1)}, f32[8,128]{1,0:T(8,128)S(1)}, u32[]{:S(2)}, u32[]{:S(2)}) collective-permute-start(f32[8,128]{1,0:T(8,128)S(1)} %get-tuple-element.18), channel_id=1, source_target_pairs={{0,136},{1,145},{2,154},{3,163},{4,172},{5,181},{6,190},{7,199},{8... | collective-permute-start | bytes 12296 | tf_op jit(solution)/shard_map/z_shift/ppermute | solution.py:186

commit v5 on v3

--- a/solution.py
+++ b/solution.py
@@ -14,6 +14,7 @@
 LARGE = 53 * 10**6
 ALL = ("outer", "z", "core", "rep")
 PLANE = ("outer", "core", "rep")
+ROW = ("core", "rep")
 PEERS = ("outer", "rep")
 
 
@@ -46,20 +47,24 @@
     ]
     for send in sends:
         send.start()
-    lane = lax.broadcasted_iota(jnp.int32, note_ref.shape, 1)
+    lane = lax.broadcasted_iota(jnp.int32, note_ref.shape[1:], 1)
     note = jnp.where(lane == 0, jnp.sum(squares), 0.0)
     for k, entry in enumerate([used] + where):
         note = jnp.where(lane == 1 + k, entry.astype(jnp.float32), note)
-    note_ref[...] = note
+    note_ref[...] = jnp.broadcast_to(note[None], note_ref.shape)
     for send in sends:
         send.wait()
 
 
-def column_kernel(column_ref, note_ref, notes_ref):
-    total = jnp.sum(column_ref[...], axis=0, keepdims=True)
-    note = note_ref[...]
+def row_kernel(notes_ref, sum_ref):
+    total = jnp.sum(notes_ref[...], axis=0)
+    sum_ref[...] = jnp.broadcast_to(total[:, 0:1], total.shape)
+
+
+def mix_kernel(other_ref, note_ref, notes_ref):
+    note = note_ref[0]
     lane = lax.broadcasted_iota(jnp.int32, note.shape, 1)
-    note = jnp.where(lane == 0, total, note)
+    note = jnp.where(lane == 0, other_ref[...], note)
     notes_ref[...] = jnp.broadcast_to(note[None], notes_ref.shape)
 
 
@@ -108,18 +113,18 @@
     _, count, side, _ = master.shape
     shards = outers * reps
     plane = shards * cores
-    limit = 0.25 * side * math.sqrt(count * plane * chips)
+    limit = 0.25 * side * math.sqrt(count * plane * plane)
     vmem = pl.BlockSpec(memory_space=pltpu.VMEM)
     smem = pl.BlockSpec(memory_space=pltpu.SMEM)
     hbm = pl.BlockSpec(memory_space=pl.ANY)
     small = pltpu.CompilerParams(vmem_limit_bytes=SMALL)
     large = pltpu.CompilerParams(vmem_limit_bytes=LARGE)
     with jax.named_scope("pick"):
-        spread, note = pl.pallas_call(
+        spread, notes = pl.pallas_call(
             pick_kernel,
             out_shape=(
                 jax.ShapeDtypeStruct((shards, SLOTS, side, side), jnp.bfloat16),
-                jax.ShapeDtypeStruct((8, TILE), jnp.float32),
+                jax.ShapeDtypeStruct((cores * reps, 8, TILE), jnp.float32),
             ),
             in_specs=[hbm, hbm, hbm],
             out_specs=(hbm, vmem),
@@ -132,20 +137,38 @@
                 pltpu.SemaphoreType.DMA((shards,)),
             ],
         )(keep_mask, master, synced)
+    with jax.named_scope("row_sum"):
+        row_sum = pl.pallas_call(
+            row_kernel,
+            out_shape=jax.ShapeDtypeStruct((8, TILE), jnp.float32),
+            in_specs=[vmem],
+            out_specs=vmem,
+            compiler_params=small,
+        )(lax.all_to_all(notes, ROW, 0, 0, tiled=True))
+    spread, row_sum = lax.optimization_barrier((spread, row_sum))
     with jax.named_scope("gather"):
         gathered = lax.all_to_all(spread, PEERS, 0, 0, tiled=True)
         gathered = gathered.reshape(shards * SLOTS, side, side)
-    with jax.named_scope("z_sum"):
-        column = lax.all_gather(note[:1], "z", axis=0, tiled=True)
+    with jax.named_scope("z_shift"):
+        pairs = []
+        for o in range(outers):
+            for z in range(chips):
+                for c in range(cores):
+                    for r in range(reps):
+                        there = (z + (o * cores + c) * reps + r - plane // 2 + 1) % chips
+                        pairs.append(
+                            (((o * chips + z) * cores + c) * reps + r, ((o * chips + there) * cores + c) * reps + r)
+                        )
+        other = lax.ppermute(lax.psum(row_sum, "outer"), ALL, pairs)
+    other, gathered = lax.optimization_barrier((other, gathered))
+    with jax.named_scope("plane_sum"):
         notes = pl.pallas_call(
-            column_kernel,
+            mix_kernel,
             out_shape=jax.ShapeDtypeStruct((plane, 8, TILE), jnp.float32),
             in_specs=[vmem, vmem],
             out_specs=vmem,
             compiler_params=small,
-        )(column, note)
-    notes, gathered = lax.optimization_barrier((notes, gathered))
-    with jax.named_scope("plane_sum"):
+        )(other, notes)
         notes = lax.all_to_all(notes, PLANE, 0, 0, tiled=True)
         factor, table = pl.pallas_call(
             functools.partial(plane_kernel, limit, outers, reps),

time: 98.9 us -> 96.2 us (0.973)
  blocking collectives: 83.2 us -> 67.8 us
  starting transfers between devices: 7.6 us -> 19.5 us
    all_gather x1 -> x0, blocking collectives: 55.1 us -> none  [body(): column = lax.all_gather(note[:1], 'z', axis=0, tiled=True)]
    all_to_all x0 -> x1, blocking collectives: none -> 22.3 us  [body(): lax.all_to_all(notes, ROW, 0, 0, tiled=True)]
    psum x0 -> x1, blocking collectives: none -> 19.6 us  [body(): other = lax.ppermute(lax.psum(row_sum, 'outer'), ALL, pairs)]
    ppermute x0 -> x1, starting transfers between devices: none -> 15.7 us  [body(): other = lax.ppermute(lax.psum(row_sum, 'outer'), ALL, pairs)]
    all_to_all x1, starting transfers between devices: 7.6 us -> 3.72 us  [body(): gathered = lax.all_to_all(spread, PEERS, 0, 0, tiled=True)]
    all_to_all x1, blocking collectives: 28.1 us -> 25.9 us  [body(): notes = lax.all_to_all(notes, PLANE, 0, 0, tiled=True)]
  transfers between devices with their start and end apart: 1 -> 2, of which waited for: 0 -> 1; matrix products, arithmetic and copies ran while one was open for 0% -> 0% of each run, Pallas kernels for 0% -> 0%
where the time goes in v5:
time: 96.2 us; the launch traced here: 95.8 us
  blocking collectives  67.8 us (70%)
  starting transfers between devices  19.5 us (20%)
  Pallas kernels  7.76 us (8%)
    all_to_all x1, blocking collectives, body(): notes = lax.all_to_all(notes, PLANE, 0, 0, tiled=True)  25.9 us
    all_to_all x1, blocking collectives, body(): lax.all_to_all(notes, ROW, 0, 0, tiled=True)  22.3 us
    psum x1, blocking collectives, body(): other = lax.ppermute(lax.psum(row_sum, 'outer'), ALL, pairs)  19.6 us
    ppermute x1, starting transfers between devices, body(): other = lax.ppermute(lax.psum(row_sum, 'outer'), ALL, pairs)  15.7 us
    pallas_call x1, Pallas kernels, body(): pl.pallas_call(functools.partial(apply_kernel, count), out_shape=jax.Shap...  4.38 us
    all_to_all x1, starting transfers between devices, body(): gathered = lax.all_to_all(spread, PEERS, 0, 0, tiled=True)  3.72 us
    pallas_call x1, Pallas kernels, body(): pl.pallas_call(pick_kernel, out_shape=(jax.ShapeDtypeStruct((shards, SLOT...  3.18 us
  transfers between devices with their start and end apart: 2, of which 1 were waited for; matrix products, arithmetic and copies ran while one was open for 0% of the time, Pallas kernels for 0%

profile of v5, /device:TPU:1, one launch (start us, length us, event | category | flops | bytes accessed | tf_op | source)
XLA Modules:
  0.0 95.8 jit_solution(6146930537080924525)
XLA Ops:
  0.0 3.2 %pick.1 = (bf16[16,4,128,128]{3,2,1,0:T(8,128)(2,1)}, f32[8,8,128]{2,1,0:T(8,128)}) custom-call(s32[1,7]{1,0:T(1,128)} %mask_hbm.1, f32[1,7,128,128]{3,2,1,0:T(8,128)} %master_hbm.1, bf16[1,7,128,128]{3,2,1,0:T(8,128)(2,1)} %synced_hbm.1), custom_call_target="tpu_custom_call" | custom-call | tf_op jit(solution)/shard_map/pick/pallas_call | solution.py:123
  3.2 0.0 copy-start
  3.2 22.3 %all_to_all.15.notes_ref = f32[8,8,128]{2,1,0:T(8,128)S(1)} all-to-all(f32[8,8,128]{2,1,0:T(8,128)} %get-tuple-element.14.note_ref), channel_id=1, replica_groups=mesh['outer'=4,'z'=32,'core'=2,'rep'=4] {'core','rep'}, dimensions={0} | all-to-all | bytes 65536 | tf_op jit(solution)/shard_map/row_sum/all_to_all | solution.py:147
  25.5 0.1 row_sum.1
  25.6 3.7 %all-to-all-start.1 = ((bf16[16,4,128,128]{3,2,1,0:T(8,128)(2,1)}), bf16[16,4,128,128]{3,2,1,0:T(8,128)(2,1)S(1)}, u32[]{:S(2)}, u32[]{:S(2)}) async-start(bf16[16,4,128,128]{3,2,1,0:T(8,128)(2,1)} %get-tuple-element.16), calls=%async_computation.1 | async-start | bytes 4194304 | tf_op jit(solution)/shard_map/gather/all_to_all | solution.py:150
  29.3 19.6 %psum.7 = f32[8,128]{1,0:T(8,128)S(1)} all-reduce(f32[8,128]{1,0:T(8,128)S(1)} %row_sum.1), channel_id=1, replica_groups=mesh['outer'=4,'z'=32,'core'=2,'rep'=4] {'outer'}, use_global_device_ids=true, to_apply=%region_0.0 | all-reduce | flops 1024 | bytes 8192 | tf_op jit(solution)/shard_map/z_shift/psum | solution.py:162
  48.9 15.7 %collective-permute-start = (f32[8,128]{1,0:T(8,128)S(1)}, f32[8,128]{1,0:T(8,128)S(1)}, u32[]{:S(2)}, u32[]{:S(2)}) collective-permute-start(f32[8,128]{1,0:T(8,128)S(1)} %psum.7), channel_id=1, source_target_pairs={{0,136},{1,145},{2,154},{3,163},{4,172},{5,181},{6,190},{7,199},{8... | collective-permute-start | bytes 12296 | tf_op jit(solution)/shard_map/z_shift/ppermute | solution.py:162
  64.7 0.7 collective-permute-done.other_ref
  65.4 0.0 all-to-all-done.1
  65.4 0.0 copy-done
  65.4 25.9 %all_to_all.16.notes_ref = f32[32,8,128]{2,1,0:T(8,128)S(1)} all-to-all(f32[32,8,128]{2,1,0:T(8,128)S(1)} %plane_sum.2), channel_id=1, replica_groups=mesh['outer'=4,'z'=32,'core'=2,'rep'=4] {'outer','core','rep'}, dimensions={0} | all-to-all | bytes 262144 | tf_op jit(solution)/shard_map/plane_sum/all_to_all | solution.py:172
  91.3 0.1 plane_sum.3
  91.4 4.4 %apply.1 = bf16[2,128,7168]{2,1,0:T(8,128)(2,1)} custom-call(s32[16,128]{1,0:T(8,128)S(1)} %get-tuple-element.18.table_ref, f32[8,128]{1,0:T(8,128)S(1)} %get-tuple-element.19.factor_ref, bf16[64,128,128]{2,1,0:T(8,128)(2,1)S(1)} %bitcast.1, bf16[2,128,7168]{2,1,0:T(8,128)(2,1)} %resident_hbm.1), custom_call_target="tpu_custom_call" | custom-call | tf_op jit(solution)/shard_map/apply/pallas_call | solution.py:184
  (1 shorter events, 0.0 us)
Async XLA Ops:
  3.2 62.2 %copy-start = (f32[8,8,128]{2,1,0:T(8,128)S(1)}, f32[8,8,128]{2,1,0:T(8,128)}, u32[]{:S(2)}) copy-start(f32[8,8,128]{2,1,0:T(8,128)} %get-tuple-element.14.note_ref) | copy-start | bytes 98308
  25.6 39.8 %all-to-all-start.1 = ((bf16[16,4,128,128]{3,2,1,0:T(8,128)(2,1)}), bf16[16,4,128,128]{3,2,1,0:T(8,128)(2,1)S(1)}, u32[]{:S(2)}, u32[]{:S(2)}) async-start(bf16[16,4,128,128]{3,2,1,0:T(8,128)(2,1)} %get-tuple-element.16), calls=%async_computation.1 | async-start | bytes 4194304 | tf_op jit(solution)/shard_map/gather/all_to_all | solution.py:150
  48.9 16.5 %collective-permute-start = (f32[8,128]{1,0:T(8,128)S(1)}, f32[8,128]{1,0:T(8,128)S(1)}, u32[]{:S(2)}, u32[]{:S(2)}) collective-permute-start(f32[8,128]{1,0:T(8,128)S(1)} %psum.7), channel_id=1, source_target_pairs={{0,136},{1,145},{2,154},{3,163},{4,172},{5,181},{6,190},{7,199},{8... | collective-permute-start | bytes 12296 | tf_op jit(solution)/shard_map/z_shift/ppermute | solution.py:162

commit v6 on v5

--- a/solution.py
+++ b/solution.py
@@ -61,10 +61,12 @@
     sum_ref[...] = jnp.broadcast_to(total[:, 0:1], total.shape)
 
 
-def mix_kernel(other_ref, note_ref, notes_ref):
+def mix_kernel(note_ref, *refs):
+    *other_refs, notes_ref = refs
+    others = sum(ref[...] for ref in other_refs)
     note = note_ref[0]
     lane = lax.broadcasted_iota(jnp.int32, note.shape, 1)
-    note = jnp.where(lane == 0, other_ref[...], note)
+    note = jnp.where(lane == 0, others, note)
     notes_ref[...] = jnp.broadcast_to(note[None], notes_ref.shape)
 
 
@@ -113,7 +115,9 @@
     _, count, side, _ = master.shape
     shards = outers * reps
     plane = shards * cores
-    limit = 0.25 * side * math.sqrt(count * plane * plane)
+    row = cores * reps
+    fetches = max(1, chips // row)
+    limit = 0.25 * side * math.sqrt(count * plane * row * fetches)
     vmem = pl.BlockSpec(memory_space=pltpu.VMEM)
     smem = pl.BlockSpec(memory_space=pltpu.SMEM)
     hbm = pl.BlockSpec(memory_space=pl.ANY)
@@ -150,25 +154,29 @@
         gathered = lax.all_to_all(spread, PEERS, 0, 0, tiled=True)
         gathered = gathered.reshape(shards * SLOTS, side, side)
     with jax.named_scope("z_shift"):
-        pairs = []
-        for o in range(outers):
-            for z in range(chips):
-                for c in range(cores):
-                    for r in range(reps):
-                        there = (z + (o * cores + c) * reps + r - plane // 2 + 1) % chips
-                        pairs.append(
-                            (((o * chips + z) * cores + c) * reps + r, ((o * chips + there) * cores + c) * reps + r)
-                        )
-        other = lax.ppermute(lax.psum(row_sum, "outer"), ALL, pairs)
-    other, gathered = lax.optimization_barrier((other, gathered))
+        others = []
+        for k in range(fetches):
+            pairs = []
+            for o in range(outers):
+                for z in range(chips):
+                    for c in range(cores):
+                        for r in range(reps):
+                            p = c * reps + r
+                            away = k * row // 2 + p // 2 + 1 if p % 2 else -(k * row // 2 + p // 2)
+                            there = (z + away) % chips
+                            pairs.append(
+                                (((o * chips + z) * cores + c) * reps + r, ((o * chips + there) * cores + c) * reps + r)
+                            )
+            others.append(lax.ppermute(row_sum, ALL, pairs))
+    others, gathered = lax.optimization_barrier((others, gathered))
     with jax.named_scope("plane_sum"):
         notes = pl.pallas_call(
             mix_kernel,
             out_shape=jax.ShapeDtypeStruct((plane, 8, TILE), jnp.float32),
-            in_specs=[vmem, vmem],
+            in_specs=[vmem] * (fetches + 1),
             out_specs=vmem,
             compiler_params=small,
-        )(other, notes)
+        )(notes, *others)
         notes = lax.all_to_all(notes, PLANE, 0, 0, tiled=True)
         factor, table = pl.pallas_call(
             functools.partial(plane_kernel, limit, outers, reps),

time: 96.2 us -> 87.5 us (0.910)
  blocking collectives: 67.8 us -> 42.6 us
  starting transfers between devices: 19.5 us -> 31.7 us
  waiting for transfers between devices: 0.74 us -> 4.95 us
    psum x1 -> x0, blocking collectives: 19.6 us -> none  [body(): other = lax.ppermute(lax.psum(row_sum, 'outer'), ALL, pairs)]
    ppermute x1 -> x4, starting transfers between devices: 15.7 us -> 28 us  [body(): others.append(lax.ppermute(row_sum, ALL, pairs))]
    all_to_all x1, blocking collectives: 25.9 us -> 20.3 us  [body(): notes = lax.all_to_all(notes, PLANE, 0, 0, tiled=True)]
    ppermute x1 -> x4, waiting for transfers between devices: 0.73 us -> 4.24 us  [body(): others.append(lax.ppermute(row_sum, ALL, pairs))]
  transfers between devices with their start and end apart: 2 -> 5, of which waited for: 1 -> 2; matrix products, arithmetic and copies ran while one was open for 0% -> 0% of each run, Pallas kernels for 0% -> 0%
where the time goes in v6:
time: 87.5 us; the launch traced here: 87 us
  blocking collectives  42.6 us (49%)
  starting transfers between devices  31.7 us (36%)
  Pallas kernels  7.72 us (9%)
  waiting for transfers between devices  4.95 us (6%)
    ppermute x4, starting transfers between devices, body(): others.append(lax.ppermute(row_sum, ALL, pairs))  28 us
    all_to_all x1, blocking collectives, body(): lax.all_to_all(notes, ROW, 0, 0, tiled=True)  22.3 us
    all_to_all x1, blocking collectives, body(): notes = lax.all_to_all(notes, PLANE, 0, 0, tiled=True)  20.3 us
    pallas_call x1, Pallas kernels, body(): pl.pallas_call(functools.partial(apply_kernel, count), out_shape=jax.Shap...  4.33 us
    ppermute x4, waiting for transfers between devices, body(): others.append(lax.ppermute(row_sum, ALL, pairs))  4.24 us
    all_to_all x1, starting transfers between devices, body(): gathered = lax.all_to_all(spread, PEERS, 0, 0, tiled=True)  3.72 us
    pallas_call x1, Pallas kernels, body(): pl.pallas_call(pick_kernel, out_shape=(jax.ShapeDtypeStruct((shards, SLOT...  3.19 us
  transfers between devices with their start and end apart: 5, of which 2 were waited for; matrix products, arithmetic and copies ran while one was open for 0% of the time, Pallas kernels for 0%

profile of v6, /device:TPU:1, one launch (start us, length us, event | category | flops | bytes accessed | tf_op | source)
XLA Modules:
  0.0 87.0 jit_solution(5399913430831276102)
XLA Ops:
  0.0 3.2 %pick.1 = (bf16[16,4,128,128]{3,2,1,0:T(8,128)(2,1)}, f32[8,8,128]{2,1,0:T(8,128)}) custom-call(s32[1,7]{1,0:T(1,128)} %mask_hbm.1, f32[1,7,128,128]{3,2,1,0:T(8,128)} %master_hbm.1, bf16[1,7,128,128]{3,2,1,0:T(8,128)(2,1)} %synced_hbm.1), custom_call_target="tpu_custom_call" | custom-call | tf_op jit(solution)/shard_map/pick/pallas_call | solution.py:127
  3.2 0.0 copy-start
  3.2 22.3 %all_to_all.15.notes_ref = f32[8,8,128]{2,1,0:T(8,128)S(1)} all-to-all(f32[8,8,128]{2,1,0:T(8,128)} %get-tuple-element.16.note_ref), channel_id=1, replica_groups=mesh['outer'=4,'z'=32,'core'=2,'rep'=4] {'core','rep'}, dimensions={0} | all-to-all | bytes 65536 | tf_op jit(solution)/shard_map/row_sum/all_to_all | solution.py:151
  25.5 0.1 row_sum.1
  25.6 3.7 %all-to-all-start.1 = ((bf16[16,4,128,128]{3,2,1,0:T(8,128)(2,1)}), bf16[16,4,128,128]{3,2,1,0:T(8,128)(2,1)S(1)}, u32[]{:S(2)}, u32[]{:S(2)}) async-start(bf16[16,4,128,128]{3,2,1,0:T(8,128)(2,1)} %get-tuple-element.19), calls=%async_computation.1 | async-start | bytes 4194304 | tf_op jit(solution)/shard_map/gather/all_to_all | solution.py:154
  29.3 17.4 %collective-permute-start.3 = (f32[8,128]{1,0:T(8,128)S(1)}, f32[8,128]{1,0:T(8,128)S(1)}, u32[]{:S(2)}, u32[]{:S(2)}) collective-permute-start(f32[8,128]{1,0:T(8,128)S(1)} %row_sum.1), channel_id=1, source_target_pairs={{0,160},{1,105},{2,154},{3,115},{4,148},{5,125},{6,142},{7,135},{8... | collective-permute-start | bytes 12296 | tf_op jit(solution)/shard_map/z_shift/ppermute | solution.py:170
  46.7 1.9 %collective-permute-start.2 = (f32[8,128]{1,0:T(8,128)S(1)}, f32[8,128]{1,0:T(8,128)S(1)}, u32[]{:S(2)}, u32[]{:S(2)}) collective-permute-start(f32[8,128]{1,0:T(8,128)S(1)} %row_sum.1), channel_id=1, source_target_pairs={{0,192},{1,73},{2,186},{3,83},{4,180},{5,93},{6,174},{7,103},{8,20... | collective-permute-start | bytes 12296 | tf_op jit(solution)/shard_map/z_shift/ppermute | solution.py:170
  48.7 3.1 %collective-permute-start.1 = (f32[8,128]{1,0:T(8,128)S(1)}, f32[8,128]{1,0:T(8,128)S(1)}, u32[]{:S(2)}, u32[]{:S(2)}) collective-permute-start(f32[8,128]{1,0:T(8,128)S(1)} %row_sum.1), channel_id=1, source_target_pairs={{0,224},{1,41},{2,218},{3,51},{4,212},{5,61},{6,206},{7,71},{8,232... | collective-permute-start | bytes 12296 | tf_op jit(solution)/shard_map/z_shift/ppermute | solution.py:170
  51.8 5.6 %collective-permute-start = (f32[8,128]{1,0:T(8,128)S(1)}, f32[8,128]{1,0:T(8,128)S(1)}, u32[]{:S(2)}, u32[]{:S(2)}) collective-permute-start(f32[8,128]{1,0:T(8,128)S(1)} %row_sum.1), channel_id=1, source_target_pairs={{0,0},{1,9},{2,250},{3,19},{4,244},{5,29},{6,238},{7,39},{8,8},{9,... | collective-permute-start | bytes 12296 | tf_op jit(solution)/shard_map/z_shift/ppermute | solution.py:170
  57.4 0.0 collective-permute-done.3.refs_3_
  57.4 4.2 %collective-permute-done.2.refs_2_ = f32[8,128]{1,0:T(8,128)S(1)} collective-permute-done((f32[8,128]{1,0:T(8,128)S(1)}, f32[8,128]{1,0:T(8,128)S(1)}, u32[]{:S(2)}, u32[]{:S(2)}) %collective-permute-start.2) | collective-permute-done | bytes 4128 | tf_op jit(solution)/shard_map/z_shift/ppermute | solution.py:170
  61.6 0.0 collective-permute-done.1.refs_1_
  61.6 0.0 collective-permute-done.refs_0_
  61.6 0.7 all-to-all-done.1
  62.3 0.0 copy-done
  62.3 20.3 %all_to_all.16.notes_ref = f32[32,8,128]{2,1,0:T(8,128)S(1)} all-to-all(f32[32,8,128]{2,1,0:T(8,128)S(1)} %plane_sum.2), channel_id=1, replica_groups=mesh['outer'=4,'z'=32,'core'=2,'rep'=4] {'outer','core','rep'}, dimensions={0} | all-to-all | bytes 262144 | tf_op jit(solution)/shard_map/plane_sum/all_to_all | solution.py:180
  82.6 0.1 plane_sum.3
  82.7 4.3 %apply.1 = bf16[2,128,7168]{2,1,0:T(8,128)(2,1)} custom-call(s32[16,128]{1,0:T(8,128)S(1)} %get-tuple-element.24.table_ref, f32[8,128]{1,0:T(8,128)S(1)} %get-tuple-element.25.factor_ref, bf16[64,128,128]{2,1,0:T(8,128)(2,1)S(1)} %bitcast.1, bf16[2,128,7168]{2,1,0:T(8,128)(2,1)} %resident_hbm.1), custom_call_target="tpu_custom_call" | custom-call | tf_op jit(solution)/shard_map/apply/pallas_call | solution.py:192
  (1 shorter events, 0.0 us)
Async XLA Ops:
  3.2 59.1 %copy-start = (f32[8,8,128]{2,1,0:T(8,128)S(1)}, f32[8,8,128]{2,1,0:T(8,128)}, u32[]{:S(2)}) copy-start(f32[8,8,128]{2,1,0:T(8,128)} %get-tuple-element.16.note_ref) | copy-start | bytes 98308
  25.6 36.7 %all-to-all-start.1 = ((bf16[16,4,128,128]{3,2,1,0:T(8,128)(2,1)}), bf16[16,4,128,128]{3,2,1,0:T(8,128)(2,1)S(1)}, u32[]{:S(2)}, u32[]{:S(2)}) async-start(bf16[16,4,128,128]{3,2,1,0:T(8,128)(2,1)} %get-tuple-element.19), calls=%async_computation.1 | async-start | bytes 4194304 | tf_op jit(solution)/shard_map/gather/all_to_all | solution.py:154
  29.3 28.0 %collective-permute-start.3 = (f32[8,128]{1,0:T(8,128)S(1)}, f32[8,128]{1,0:T(8,128)S(1)}, u32[]{:S(2)}, u32[]{:S(2)}) collective-permute-start(f32[8,128]{1,0:T(8,128)S(1)} %row_sum.1), channel_id=1, source_target_pairs={{0,160},{1,105},{2,154},{3,115},{4,148},{5,125},{6,142},{7,135},{8... | collective-permute-start | bytes 12296 | tf_op jit(solution)/shard_map/z_shift/ppermute | solution.py:170
  46.7 14.9 %collective-permute-start.2 = (f32[8,128]{1,0:T(8,128)S(1)}, f32[8,128]{1,0:T(8,128)S(1)}, u32[]{:S(2)}, u32[]{:S(2)}) collective-permute-start(f32[8,128]{1,0:T(8,128)S(1)} %row_sum.1), channel_id=1, source_target_pairs={{0,192},{1,73},{2,186},{3,83},{4,180},{5,93},{6,174},{7,103},{8,20... | collective-permute-start | bytes 12296 | tf_op jit(solution)/shard_map/z_shift/ppermute | solution.py:170
  48.7 12.9 %collective-permute-start.1 = (f32[8,128]{1,0:T(8,128)S(1)}, f32[8,128]{1,0:T(8,128)S(1)}, u32[]{:S(2)}, u32[]{:S(2)}) collective-permute-start(f32[8,128]{1,0:T(8,128)S(1)} %row_sum.1), channel_id=1, source_target_pairs={{0,224},{1,41},{2,218},{3,51},{4,212},{5,61},{6,206},{7,71},{8,232... | collective-permute-start | bytes 12296 | tf_op jit(solution)/shard_map/z_shift/ppermute | solution.py:170
  51.8 9.9 %collective-permute-start = (f32[8,128]{1,0:T(8,128)S(1)}, f32[8,128]{1,0:T(8,128)S(1)}, u32[]{:S(2)}, u32[]{:S(2)}) collective-permute-start(f32[8,128]{1,0:T(8,128)S(1)} %row_sum.1), channel_id=1, source_target_pairs={{0,0},{1,9},{2,250},{3,19},{4,244},{5,29},{6,238},{7,39},{8,8},{9,... | collective-permute-start | bytes 12296 | tf_op jit(solution)/shard_map/z_shift/ppermute | solution.py:170

commit v7 on v3

--- a/solution.py
+++ b/solution.py
@@ -12,12 +12,13 @@
 TILE = 128
 SMALL = 4 * 2**20
 LARGE = 53 * 10**6
+PICK = 568 * 10**5
 ALL = ("outer", "z", "core", "rep")
 PLANE = ("outer", "core", "rep")
 PEERS = ("outer", "rep")
 
 
-def pick_kernel(mask_hbm, master_hbm, synced_hbm, spread_hbm, note_ref, mask_ref, master_ref, synced_ref, tiles_ref, sem, out_sem):
+def pick_kernel(mask_hbm, master_hbm, synced_hbm, spread_hbm, notes_ref, mask_ref, master_ref, synced_ref, tiles_ref, sem, out_sem):
     loads = [
         pltpu.make_async_copy(mask_hbm, mask_ref, sem.at[0]),
         pltpu.make_async_copy(master_hbm, master_ref, sem.at[1]),
@@ -46,35 +47,26 @@
     ]
     for send in sends:
         send.start()
-    lane = lax.broadcasted_iota(jnp.int32, note_ref.shape, 1)
+    lane = lax.broadcasted_iota(jnp.int32, notes_ref.shape[1:], 1)
     note = jnp.where(lane == 0, jnp.sum(squares), 0.0)
     for k, entry in enumerate([used] + where):
         note = jnp.where(lane == 1 + k, entry.astype(jnp.float32), note)
-    note_ref[...] = note
+    notes_ref[...] = jnp.broadcast_to(note[None], notes_ref.shape)
     for send in sends:
         send.wait()
 
 
-def column_kernel(column_ref, note_ref, notes_ref):
-    total = jnp.sum(column_ref[...], axis=0, keepdims=True)
-    note = note_ref[...]
-    lane = lax.broadcasted_iota(jnp.int32, note.shape, 1)
-    note = jnp.where(lane == 0, total, note)
-    notes_ref[...] = jnp.broadcast_to(note[None], notes_ref.shape)
-
-
-def plane_kernel(limit, outers, reps, notes_ref, factor_ref, table_ref):
+def plane_kernel(outers, reps, notes_ref, sum_ref, table_ref):
     core = lax.axis_index("core")
     total = jnp.sum(notes_ref[...], axis=0)
-    total = jnp.broadcast_to(total[:, 0:1], total.shape)
-    factor_ref[...] = jnp.minimum(jnp.float32(1.0), limit / jnp.sqrt(total))
+    sum_ref[...] = jnp.broadcast_to(total[:, 0:1], total.shape)
     lane = lax.broadcasted_iota(jnp.int32, (reps, TILE), 1)
     for y in range(outers):
         mine = notes_ref[pl.ds((y * 2 + core) * reps, reps), 0, :]
         table_ref[y * reps:(y + 1) * reps, :] = jnp.where(lane == 0, 0.0, mine).astype(jnp.int32)
 
 
-def apply_kernel(count, table_ref, factor_ref, tiles_ref, resident_hbm, out_hbm, rows_ref, in_sem, out_sem):
+def apply_kernel(limit, count, table_ref, sums_ref, tiles_ref, resident_hbm, out_hbm, rows_ref, in_sem, out_sem):
     shards = table_ref.shape[0]
     wide = count * TILE
     per_layer = resident_hbm.shape[2] // wide
@@ -86,7 +78,8 @@
     stores = [pltpu.make_async_copy(block(rows_ref, j), block(out_hbm, j), out_sem.at[j]) for j in range(shards)]
     for load in loads:
         load.start()
-    factor = factor_ref[...][None]
+    total = jnp.sum(sums_ref[...], axis=0)
+    factor = jnp.minimum(jnp.float32(1.0), limit / jnp.sqrt(total))[None]
     for j in range(shards):
         loads[j].wait()
 
@@ -108,18 +101,17 @@
     _, count, side, _ = master.shape
     shards = outers * reps
     plane = shards * cores
-    limit = 0.25 * side * math.sqrt(count * plane * chips)
     vmem = pl.BlockSpec(memory_space=pltpu.VMEM)
     smem = pl.BlockSpec(memory_space=pltpu.SMEM)
     hbm = pl.BlockSpec(memory_space=pl.ANY)
     small = pltpu.CompilerParams(vmem_limit_bytes=SMALL)
     large = pltpu.CompilerParams(vmem_limit_bytes=LARGE)
     with jax.named_scope("pick"):
-        spread, note = pl.pallas_call(
+        spread, notes = pl.pallas_call(
             pick_kernel,
             out_shape=(
                 jax.ShapeDtypeStruct((shards, SLOTS, side, side), jnp.bfloat16),
-                jax.ShapeDtypeStruct((8, TILE), jnp.float32),
+                jax.ShapeDtypeStruct((plane, 8, TILE), jnp.float32),
             ),
             in_specs=[hbm, hbm, hbm],
             out_specs=(hbm, vmem),
@@ -131,24 +123,12 @@
                 pltpu.SemaphoreType.DMA((3,)),
                 pltpu.SemaphoreType.DMA((shards,)),
             ],
+            compiler_params=pltpu.CompilerParams(vmem_limit_bytes=PICK),
         )(keep_mask, master, synced)
-    with jax.named_scope("gather"):
-        gathered = lax.all_to_all(spread, PEERS, 0, 0, tiled=True)
-        gathered = gathered.reshape(shards * SLOTS, side, side)
-    with jax.named_scope("z_sum"):
-        column = lax.all_gather(note[:1], "z", axis=0, tiled=True)
-        notes = pl.pallas_call(
-            column_kernel,
-            out_shape=jax.ShapeDtypeStruct((plane, 8, TILE), jnp.float32),
-            in_specs=[vmem, vmem],
-            out_specs=vmem,
-            compiler_params=small,
-        )(column, note)
-    notes, gathered = lax.optimization_barrier((notes, gathered))
     with jax.named_scope("plane_sum"):
         notes = lax.all_to_all(notes, PLANE, 0, 0, tiled=True)
-        factor, table = pl.pallas_call(
-            functools.partial(plane_kernel, limit, outers, reps),
+        plane_total, table = pl.pallas_call(
+            functools.partial(plane_kernel, outers, reps),
             out_shape=(
                 jax.ShapeDtypeStruct((8, TILE), jnp.float32),
                 jax.ShapeDtypeStruct((shards, TILE), jnp.int32),
@@ -157,9 +137,29 @@
             out_specs=(vmem, vmem),
             compiler_params=small,
         )(notes)
+    spread, plane_total = lax.optimization_barrier((spread, plane_total))
+    with jax.named_scope("gather"):
+        gathered = lax.all_to_all(spread, PEERS, 0, 0, tiled=True)
+        gathered = gathered.reshape(shards * SLOTS, side, side)
+    with jax.named_scope("z_shift"):
+        pairs = []
+        for o in range(outers):
+            for z in range(chips):
+                for c in range(cores):
+                    for r in range(reps):
+                        there = (z + (o * cores + c) * reps + r - plane // 2 + 1) % chips
+                        pairs.append(
+                            (((o * chips + z) * cores + c) * reps + r, ((o * chips + there) * cores + c) * reps + r)
+                        )
+        other = lax.ppermute(plane_total, ALL, pairs)
+    other, gathered = lax.optimization_barrier((other, gathered))
+    with jax.named_scope("z_sum"):
+        sums = lax.all_to_all(jnp.broadcast_to(other[None], (plane, 8, TILE)), PLANE, 0, 0, tiled=True)
+    limit = 0.25 * side * math.sqrt(count * plane * chips)
+    limit = limit * math.sqrt(plane / chips)
     with jax.named_scope("apply"):
         return pl.pallas_call(
-            functools.partial(apply_kernel, count),
+            functools.partial(apply_kernel, limit, count),
             out_shape=jax.ShapeDtypeStruct(resident.shape, resident.dtype),
             in_specs=[smem, vmem, vmem, hbm],
             out_specs=hbm,
@@ -169,7 +169,7 @@
                 pltpu.SemaphoreType.DMA((shards,)),
             ],
             compiler_params=large,
-        )(table, factor, gathered, resident)
+        )(table, sums, gathered, resident)
 
 
 def solution(mesh):

time: 98.9 us -> 82.6 us (0.84)
  blocking collectives: 83.2 us -> 37.6 us
  waiting for transfers between devices: 0.01 us -> 17.2 us
  starting transfers between devices: 7.6 us -> 19.8 us
    all_gather x1 -> x0, blocking collectives: 55.1 us -> none  [body(): column = lax.all_gather(note[:1], 'z', axis=0, tiled=True)]
    all_to_all x1, waiting for transfers between devices: 0.01 us -> 16.5 us  [body(): gathered = lax.all_to_all(spread, PEERS, 0, 0, tiled=True)]
    ppermute x0 -> x1, starting transfers between devices: none -> 16.1 us  [body(): other = lax.ppermute(plane_total, ALL, pairs)]
    all_to_all x0 -> x1, blocking collectives: none -> 12.2 us  [body(): lax.all_to_all(jnp.broadcast_to(other[None], (plane, 8, TILE)), PLANE, 0,...]
    all_to_all x1, starting transfers between devices: 7.6 us -> 3.72 us  [body(): gathered = lax.all_to_all(spread, PEERS, 0, 0, tiled=True)]
    all_to_all x1, blocking collectives: 28.1 us -> 25.4 us  [body(): notes = lax.all_to_all(notes, PLANE, 0, 0, tiled=True)]
    pallas_call x3 -> x2, Pallas kernels: 4.58 us -> 4.41 us  [the longest x1 4.31 us: body(): pl.pallas_call(functools.partial(apply_kernel, limit, count), out_shape=j...]
  transfers between devices with their start and end apart: 1 -> 2, of which waited for: 0 -> 2; matrix products, arithmetic and copies ran while one was open for 0% -> 0% of each run, Pallas kernels for 0% -> 0%
where the time goes in v7:
time: 82.6 us; the launch traced here: 82.2 us
  blocking collectives  37.6 us (46%)
  starting transfers between devices  19.8 us (24%)
  waiting for transfers between devices  17.2 us (21%)
  Pallas kernels  7.64 us (9%)
    all_to_all x1, blocking collectives, body(): notes = lax.all_to_all(notes, PLANE, 0, 0, tiled=True)  25.4 us
    all_to_all x1, waiting for transfers between devices, body(): gathered = lax.all_to_all(spread, PEERS, 0, 0, tiled=True)  16.5 us
    ppermute x1, starting transfers between devices, body(): other = lax.ppermute(plane_total, ALL, pairs)  16.1 us
    all_to_all x1, blocking collectives, body(): lax.all_to_all(jnp.broadcast_to(other[None], (plane, 8, TILE)), PLANE, 0,...  12.2 us
    pallas_call x1, Pallas kernels, body(): pl.pallas_call(functools.partial(apply_kernel, limit, count), out_shape=j...  4.31 us
    all_to_all x1, starting transfers between devices, body(): gathered = lax.all_to_all(spread, PEERS, 0, 0, tiled=True)  3.72 us
    pallas_call x1, Pallas kernels, body(): pl.pallas_call(pick_kernel, out_shape=(jax.ShapeDtypeStruct((shards, SLOT...  3.23 us
  transfers between devices with their start and end apart: 2, of which 2 were waited for; matrix products, arithmetic and copies ran while one was open for 0% of the time, Pallas kernels for 0%

profile of v7, /device:TPU:1, one launch (start us, length us, event | category | flops | bytes accessed | tf_op | source)
XLA Modules:
  0.0 82.2 jit_solution(14635192922680351845)
XLA Ops:
  0.0 3.2 %pick.1 = (bf16[16,4,128,128]{3,2,1,0:T(8,128)(2,1)}, f32[32,8,128]{2,1,0:T(8,128)}) custom-call(s32[1,7]{1,0:T(1,128)} %mask_hbm.1, f32[1,7,128,128]{3,2,1,0:T(8,128)} %master_hbm.1, bf16[1,7,128,128]{3,2,1,0:T(8,128)(2,1)} %synced_hbm.1), custom_call_target="tpu_custom_call" | custom-call | tf_op jit(solution)/shard_map/pick/pallas_call | solution.py:110
  3.2 25.4 %all_to_all.15.notes_ref = f32[32,8,128]{2,1,0:T(8,128)S(1)} all-to-all(f32[32,8,128]{2,1,0:T(8,128)} %get-tuple-element.13), channel_id=1, replica_groups=mesh['outer'=4,'z'=32,'core'=2,'rep'=4] {'outer','core','rep'}, dimensions={0} | all-to-all | bytes 262144 | tf_op jit(solution)/shard_map/plane_sum/all_to_all | solution.py:129
  28.6 0.1 plane_sum.1
  28.7 3.7 %all-to-all-start.1 = ((bf16[16,4,128,128]{3,2,1,0:T(8,128)(2,1)}), bf16[16,4,128,128]{3,2,1,0:T(8,128)(2,1)S(1)}, u32[]{:S(2)}, u32[]{:S(2)}) async-start(bf16[16,4,128,128]{3,2,1,0:T(8,128)(2,1)} %get-tuple-element.18), calls=%async_computation.1 | async-start | bytes 4194304 | tf_op jit(solution)/shard_map/gather/all_to_all | solution.py:142
  32.5 16.1 %collective-permute-start = (f32[8,128]{1,0:T(8,128)S(1)}, f32[8,128]{1,0:T(8,128)S(1)}, u32[]{:S(2)}, u32[]{:S(2)}) collective-permute-start(f32[8,128]{1,0:T(8,128)S(1)} %get-tuple-element.17), channel_id=1, source_target_pairs={{0,136},{1,145},{2,154},{3,163},{4,172},{5,181},{6,190},{7,199},{8... | collective-permute-start | bytes 12296 | tf_op jit(solution)/shard_map/z_shift/ppermute | solution.py:154
  48.6 0.7 collective-permute-done
  49.3 16.5 %all-to-all-done.1 = bf16[16,4,128,128]{3,2,1,0:T(8,128)(2,1)S(1)} async-done(((bf16[16,4,128,128]{3,2,1,0:T(8,128)(2,1)}), bf16[16,4,128,128]{3,2,1,0:T(8,128)(2,1)S(1)}, u32[]{:S(2)}, u32[]{:S(2)}) %all-to-all-start.1) | async-done | bytes 2097184 | tf_op jit(solution)/shard_map/gather/all_to_all | solution.py:142
  65.8 12.2 %all_to_all.16.sums_ref = f32[32,8,128]{2,1,0:T(8,128)S(1)} all-to-all(f32[32,8,128]{2,1,0:T(8,128)S(1)} %broadcast_in_dim.2), channel_id=1, replica_groups=mesh['outer'=4,'z'=32,'core'=2,'rep'=4] {'outer','core','rep'}, dimensions={0} | all-to-all | bytes 262144 | tf_op jit(solution)/shard_map/z_sum/all_to_all | solution.py:157
  77.9 4.3 %apply.1 = bf16[2,128,7168]{2,1,0:T(8,128)(2,1)} custom-call(s32[16,128]{1,0:T(8,128)S(1)} %get-tuple-element.14.table_ref, f32[32,8,128]{2,1,0:T(8,128)S(1)} %all_to_all.16.sums_ref, bf16[64,128,128]{2,1,0:T(8,128)(2,1)S(1)} %bitcast.1, bf16[2,128,7168]{2,1,0:T(8,128)(2,1)} %resident_hbm.1), custom_call_target="tpu_custom_call" | custom-call | tf_op jit(solution)/shard_map/apply/pallas_call | solution.py:161
  (1 shorter events, 0.0 us)
Async XLA Ops:
  28.7 37.0 %all-to-all-start.1 = ((bf16[16,4,128,128]{3,2,1,0:T(8,128)(2,1)}), bf16[16,4,128,128]{3,2,1,0:T(8,128)(2,1)S(1)}, u32[]{:S(2)}, u32[]{:S(2)}) async-start(bf16[16,4,128,128]{3,2,1,0:T(8,128)(2,1)} %get-tuple-element.18), calls=%async_computation.1 | async-start | bytes 4194304 | tf_op jit(solution)/shard_map/gather/all_to_all | solution.py:142
  32.5 16.8 %collective-permute-start = (f32[8,128]{1,0:T(8,128)S(1)}, f32[8,128]{1,0:T(8,128)S(1)}, u32[]{:S(2)}, u32[]{:S(2)}) collective-permute-start(f32[8,128]{1,0:T(8,128)S(1)} %get-tuple-element.17), channel_id=1, source_target_pairs={{0,136},{1,145},{2,154},{3,163},{4,172},{5,181},{6,190},{7,199},{8... | collective-permute-start | bytes 12296 | tf_op jit(solution)/shard_map/z_shift/ppermute | solution.py:154

commit v8 on v7

v8 whole, which is shorter than its diff:
```python
import functools
import math

import jax
import jax.numpy as jnp
from jax import lax
from jax.experimental import pallas as pl
from jax.experimental.pallas import tpu as pltpu
from jax.sharding import Mesh, PartitionSpec as P

SLOTS = 4
LATER = SLOTS - 1
TILE = 128
SMALL = 4 * 2**20
LARGE = 53 * 10**6
PICK = 568 * 10**5
ALL = ("outer", "z", "core", "rep")
PLANE = ("outer", "core", "rep")
PEERS = ("outer", "rep")


def pick_kernel(
    mask_hbm, master_hbm, synced_hbm, first_hbm, later_hbm, mask_ref, master_ref, synced_ref, first_ref, later_ref, sem, out_sem
):
    shards = later_hbm.shape[0]
    loads = [
        pltpu.make_async_copy(mask_hbm, mask_ref, sem.at[0]),
        pltpu.make_async_copy(master_hbm, master_ref, sem.at[1]),
        pltpu.make_async_copy(synced_hbm, synced_ref, sem.at[2]),
    ]
    for load in loads:
        load.start()
    loads[0].wait()
    where = [jnp.int32(0)] * SLOTS
    used = jnp.int32(0)
    for i in range(mask_ref.shape[1]):
        listed = mask_ref[0, i] > 0
        for s in range(SLOTS):
            where[s] = jnp.where(listed & (used == s), i, where[s])
        used = used + listed.astype(jnp.int32)
    for load in loads[1:]:
        load.wait()
    squares = jnp.zeros((8, TILE), jnp.float32)
    for s in range(SLOTS):
        delta = (master_ref[0, where[s]] - synced_ref[0, where[s]].astype(jnp.float32)).astype(jnp.bfloat16)
        if s == 0:
            first_ref[0:TILE] = delta
        else:
            later_ref[s - 1] = delta
        wide = jnp.where(used > s, delta.astype(jnp.float32), 0.0)
        squares = squares + jnp.sum((wide * wide).reshape(-1, 8, TILE), axis=0)
    sends = [pltpu.make_async_copy(later_ref, later_hbm.at[j], out_sem.at[0, j]) for j in range(shards)]
    for send in sends:
        send.start()
    lane = lax.broadcasted_iota(jnp.int32, (16, TILE), 1)
    total = jnp.full((16, TILE), jnp.sum(squares), jnp.float32)
    high = total.astype(jnp.bfloat16).astype(jnp.float32)
    middle = (total - high).astype(jnp.bfloat16).astype(jnp.float32)
    low = total - high - middle
    note = jnp.where(lane == 0, high, jnp.where(lane == 8, middle, jnp.where(lane == 9, low, 0.0)))
    for k, entry in enumerate([used] + where):
        note = jnp.where(lane == 1 + k, entry.astype(jnp.float32), note)
    first_ref[TILE:TILE + 16] = note.astype(jnp.bfloat16)
    firsts = [pltpu.make_async_copy(first_ref, first_hbm.at[j], out_sem.at[1, j]) for j in range(shards)]
    for send in firsts:
        send.start()
    for send in sends + firsts:
        send.wait()


def plane_kernel(first_ref, sum_ref, table_ref):
    shards = first_ref.shape[0]
    lane = lax.broadcasted_iota(jnp.int32, (16, TILE), 1)
    part = (lane == 0) | (lane == 8) | (lane == 9)
    total = jnp.zeros((16, TILE), jnp.float32)
    for j in range(shards):
        note = first_ref[j, TILE:TILE + 16].astype(jnp.float32)
        total = total + jnp.sum(jnp.where(part, note, 0.0), axis=1, keepdims=True)
        table_ref[j:j + 1, :] = jnp.where(part, 0.0, note)[0:1].astype(jnp.int32)
    sum_ref[...] = total[0:8]


def apply_kernel(
    limit, count, table_ref, sums_ref, first_hbm, later_ref, resident_hbm, out_hbm, rows_ref, first_ref, in_sem, first_sem, out_sem
):
    shards = table_ref.shape[0]
    wide = count * TILE
    per_layer = resident_hbm.shape[2] // wide

    def block(ref, j):
        return ref.at[j // per_layer, :, pl.ds((j % per_layer) * wide, wide)]

    loads = [pltpu.make_async_copy(block(resident_hbm, j), block(rows_ref, j), in_sem.at[j]) for j in range(shards)]
    firsts = [
        pltpu.make_async_copy(first_hbm.at[j, pl.ds(0, TILE)], first_ref.at[j], first_sem.at[j]) for j in range(shards)
    ]
    stores = [pltpu.make_async_copy(block(rows_ref, j), block(out_hbm, j), out_sem.at[j]) for j in range(shards)]
    for first, load in zip(firsts, loads):
        first.start()
        load.start()
    total = jnp.sum(sums_ref[...], axis=0)
    factor = jnp.minimum(jnp.float32(1.0), limit / jnp.sqrt(total))[None]
    for j in range(shards):
        firsts[j].wait()
        loads[j].wait()

        def add(slot, tile):
            start = pl.multiple_of((j % per_layer) * wide + table_ref[j, 2 + slot] * TILE, TILE)
            place = (j // per_layer, slice(None), pl.ds(start, TILE))
            moved = (factor * tile.astype(jnp.float32).reshape(-1, 8, TILE)).reshape(TILE, TILE)
            rows_ref[place] = (rows_ref[place].astype(jnp.float32) + moved).astype(jnp.bfloat16)

        @pl.when(table_ref[j, 1] > 0)
        def _():
            add(0, first_ref[j])

        def later(s, _):
            add(s, later_ref[j * LATER + s - 1])
            return 0

        lax.fori_loop(1, table_ref[j, 1], later, 0)
        stores[j].start()
    for store in stores:
        store.wait()


def body(master, synced, keep_mask, resident):
    outers, chips, cores, reps = (lax.axis_size(a) for a in ALL)
    _, count, side, _ = master.shape
    shards = outers * reps
    plane = shards * cores
    fetches = max(1, chips // shards)
    limit = 0.25 * side * math.sqrt(count * plane * shards * fetches)
    vmem = pl.BlockSpec(memory_space=pltpu.VMEM)
    smem = pl.BlockSpec(memory_space=pltpu.SMEM)
    hbm = pl.BlockSpec(memory_space=pl.ANY)
    small = pltpu.CompilerParams(vmem_limit_bytes=SMALL)
    large = pltpu.CompilerParams(vmem_limit_bytes=LARGE)
    with jax.named_scope("pick"):
        first, later = pl.pallas_call(
            pick_kernel,
            out_shape=(
                jax.ShapeDtypeStruct((shards, side + 16, side), jnp.bfloat16),
                jax.ShapeDtypeStruct((shards, LATER, side, side), jnp.bfloat16),
            ),
            in_specs=[hbm, hbm, hbm],
            out_specs=(hbm, hbm),
            scratch_shapes=[
                pltpu.SMEM(keep_mask.shape, keep_mask.dtype),
                pltpu.VMEM(master.shape, master.dtype),
                pltpu.VMEM(synced.shape, synced.dtype),
                pltpu.VMEM((side + 16, side), jnp.bfloat16),
                pltpu.VMEM((LATER, side, side), jnp.bfloat16),
                pltpu.SemaphoreType.DMA((3,)),
                pltpu.SemaphoreType.DMA((2, shards)),
            ],
        )(keep_mask, master, synced)
    with jax.named_scope("first_slot"):
        first = lax.all_to_all(first, PEERS, 0, 0, tiled=True)
        plane_sum, table = pl.pallas_call(
            plane_kernel,
            out_shape=(
                jax.ShapeDtypeStruct((8, TILE), jnp.float32),
                jax.ShapeDtypeStruct((shards, TILE), jnp.int32),
            ),
            in_specs=[vmem],
            out_specs=(vmem, vmem),
            compiler_params=small,
        )(first)
    later, plane_sum = lax.optimization_barrier((later, plane_sum))
    with jax.named_scope("later_slots"):
        later = lax.all_to_all(later, PEERS, 0, 0, tiled=True)
        later = later.reshape(shards * LATER, side, side)
    with jax.named_scope("z_shift"):
        others = []
        for k in range(fetches):
            pairs = []
            for o in range(outers):
                for z in range(chips):
                    for c in range(cores):
                        for r in range(reps):
                            p = o * reps + r
                            away = k * shards // 2 + p // 2 + 1 if p % 2 else -(k * shards // 2 + p // 2)
                            there = (z + away) % chips
                            pairs.append(
                                (((o * chips + z) * cores + c) * reps + r, ((o * chips + there) * cores + c) * reps + r)
                            )
            others.append(lax.ppermute(plane_sum, ALL, pairs))
    others, later = lax.optimization_barrier((others, later))
    with jax.named_scope("z_sum"):
        sums = lax.all_to_all(jnp.broadcast_to(sum(others)[None], (plane, 8, TILE)), PLANE, 0, 0, tiled=True)
    with jax.named_scope("apply"):
        return pl.pallas_call(
            functools.partial(apply_kernel, limit, count),
            out_shape=jax.ShapeDtypeStruct(resident.shape, resident.dtype),
            in_specs=[smem, vmem, hbm, vmem, hbm],
            out_specs=hbm,
            scratch_shapes=[
                pltpu.VMEM(resident.shape, resident.dtype),
                pltpu.VMEM((shards, side, side), jnp.bfloat16),
                pltpu.SemaphoreType.DMA((shards,)),
                pltpu.SemaphoreType.DMA((shards,)),
                pltpu.SemaphoreType.DMA((shards,)),
            ],
            compiler_params=large,
        )(table, sums, first, later, resident)


def solution(mesh):
    outers, tensors, reps = mesh.devices.shape
    fine = Mesh(mesh.devices.reshape(outers, tensors // 2, 2, reps), ALL)
    head = ("z", "core")
    placed = (
        P(head, PEERS, None, None),
        P(head, PEERS, None, None),
        P(head, PEERS),
        P(None, head, None),
    )
    return jax.shard_map(
        body, mesh=fine, in_specs=placed, out_specs=P(None, head, None), check_vma=False
    )
```

time: 82.6 us -> 89.6 us (1.085)
  waiting for transfers between devices: 17.2 us -> 0.07 us
  blocking collectives: 37.6 us -> 52.7 us
  starting transfers between devices: 19.8 us -> 29 us
    all_to_all x1, waiting for transfers between devices: 16.5 us -> 0.01 us  [body(): later = lax.all_to_all(later, PEERS, 0, 0, tiled=True)]
    all_to_all x2, blocking collectives: 37.6 us -> 52.7 us  [the longest x1 35.7 us: body(): lax.all_to_all(jnp.broadcast_to(sum(others)[None], (plane, 8, TILE)), PLA...]
    ppermute x1 -> x2, starting transfers between devices: 16.1 us -> 25.3 us  [body(): others.append(lax.ppermute(plane_sum, ALL, pairs))]
  transfers between devices with their start and end apart: 2 -> 3, of which waited for: 2 -> 1; matrix products, arithmetic and copies ran while one was open for 0% -> 0% of each run, Pallas kernels for 0% -> 0%
where the time goes in v8:
time: 89.6 us; the launch traced here: 89.2 us
  blocking collectives  52.7 us (59%)
  starting transfers between devices  29 us (32%)
  Pallas kernels  7.4 us (8%)
    all_to_all x1, blocking collectives, body(): lax.all_to_all(jnp.broadcast_to(sum(others)[None], (plane, 8, TILE)), PLA...  35.7 us
    ppermute x2, starting transfers between devices, body(): others.append(lax.ppermute(plane_sum, ALL, pairs))  25.3 us
    all_to_all x1, blocking collectives, body(): first = lax.all_to_all(first, PEERS, 0, 0, tiled=True)  17 us
    pallas_call x1, Pallas kernels, body(): pl.pallas_call(functools.partial(apply_kernel, limit, count), out_shape=j...  4.58 us
    all_to_all x1, starting transfers between devices, body(): later = lax.all_to_all(later, PEERS, 0, 0, tiled=True)  3.72 us
    pallas_call x1, Pallas kernels, body(): pl.pallas_call(pick_kernel, out_shape=(jax.ShapeDtypeStruct((shards, side...  2.73 us
  transfers between devices with their start and end apart: 3, of which 1 were waited for; matrix products, arithmetic and copies ran while one was open for 0% of the time, Pallas kernels for 0%

profile of v8, /device:TPU:1, one launch (start us, length us, event | category | flops | bytes accessed | tf_op | source)
XLA Modules:
  0.0 89.2 jit_solution(13515597242057492647)
XLA Ops:
  0.0 2.7 %pick.1 = (bf16[16,144,128]{2,1,0:T(8,128)(2,1)}, bf16[16,3,128,128]{3,2,1,0:T(8,128)(2,1)}) custom-call(s32[1,7]{1,0:T(1,128)} %mask_hbm.1, f32[1,7,128,128]{3,2,1,0:T(8,128)} %master_hbm.1, bf16[1,7,128,128]{3,2,1,0:T(8,128)(2,1)} %synced_hbm.1), custom_call_target="tpu_custom_call" | custom-call | tf_op jit(solution)/shard_map/pick/pallas_call | solution.py:140
  2.7 17.0 %all_to_all.15.first_ref.first_hbm = bf16[16,144,128]{2,1,0:T(8,128)(2,1)S(1)} all-to-all(bf16[16,144,128]{2,1,0:T(8,128)(2,1)} %get-tuple-element.14), channel_id=1, replica_groups=mesh['outer'=4,'z'=32,'core'=2,'rep'=4] {'outer','rep'}, dimensions={0} | all-to-all | bytes 1179648 | tf_op jit(solution)/shard_map/first_slot/all_to_all | solution.py:159
  19.7 0.1 first_slot.1
  19.8 3.7 %all-to-all-start.1 = ((bf16[16,3,128,128]{3,2,1,0:T(8,128)(2,1)}), bf16[16,3,128,128]{3,2,1,0:T(8,128)(2,1)S(1)}, u32[]{:S(2)}, u32[]{:S(2)}) async-start(bf16[16,3,128,128]{3,2,1,0:T(8,128)(2,1)} %get-tuple-element.19), calls=%async_computation.1 | async-start | bytes 3145728 | tf_op jit(solution)/shard_map/later_slots/all_to_all | solution.py:172
  23.5 24.6 %collective-permute-start.1 = (f32[8,128]{1,0:T(8,128)S(1)}, f32[8,128]{1,0:T(8,128)S(1)}, u32[]{:S(2)}, u32[]{:S(2)}) collective-permute-start(f32[8,128]{1,0:T(8,128)S(1)} %get-tuple-element.18), channel_id=1, source_target_pairs={{0,192},{1,73},{2,186},{3,83},{4,196},{5,77},{6,190},{7,87},{8,200... | collective-permute-start | bytes 12296 | tf_op jit(solution)/shard_map/z_shift/ppermute | solution.py:188
  48.2 0.7 collective-permute-start
  48.8 0.1 collective-permute-done.1
  48.9 0.0 collective-permute-done
  48.9 0.0 all-to-all-done.1
  48.9 35.7 %all_to_all.16.sums_ref = f32[32,8,128]{2,1,0:T(8,128)S(1)} all-to-all(f32[32,8,128]{2,1,0:T(8,128)S(1)} %broadcast_in_dim.2), channel_id=1, replica_groups=mesh['outer'=4,'z'=32,'core'=2,'rep'=4] {'outer','core','rep'}, dimensions={0} | all-to-all | bytes 262144 | tf_op jit(solution)/shard_map/z_sum/all_to_all | solution.py:191
  84.7 4.6 %apply.1 = bf16[2,128,7168]{2,1,0:T(8,128)(2,1)} custom-call(s32[16,128]{1,0:T(8,128)S(1)} %get-tuple-element.15.table_ref, f32[32,8,128]{2,1,0:T(8,128)S(1)} %all_to_all.16.sums_ref, bf16[16,144,128]{2,1,0:T(8,128)(2,1)S(1)} %all_to_all.15.first_ref.first_hbm, bf16[48,128,128]{2,1,0:T(8,128)(2,1)S(1)} %bitcast.1, bf16[2,128,7168]{2,1,0:T(8,128)(2,1)} %resident_hbm.1), custom_call_target="tpu_custom_call" | custom-call | tf_op jit(solution)/shard_map/apply/pallas_call | solution.py:193
  (2 shorter events, 0.0 us)
Async XLA Ops:
  19.8 29.1 %all-to-all-start.1 = ((bf16[16,3,128,128]{3,2,1,0:T(8,128)(2,1)}), bf16[16,3,128,128]{3,2,1,0:T(8,128)(2,1)S(1)}, u32[]{:S(2)}, u32[]{:S(2)}) async-start(bf16[16,3,128,128]{3,2,1,0:T(8,128)(2,1)} %get-tuple-element.19), calls=%async_computation.1 | async-start | bytes 3145728 | tf_op jit(solution)/shard_map/later_slots/all_to_all | solution.py:172
  23.5 25.4 %collective-permute-start.1 = (f32[8,128]{1,0:T(8,128)S(1)}, f32[8,128]{1,0:T(8,128)S(1)}, u32[]{:S(2)}, u32[]{:S(2)}) collective-permute-start(f32[8,128]{1,0:T(8,128)S(1)} %get-tuple-element.18), channel_id=1, source_target_pairs={{0,192},{1,73},{2,186},{3,83},{4,196},{5,77},{6,190},{7,87},{8,200... | collective-permute-start | bytes 12296 | tf_op jit(solution)/shard_map/z_shift/ppermute | solution.py:188
  48.2 0.7 collective-permute-start

commit v9 on v8

--- a/solution.py
+++ b/solution.py
@@ -129,8 +129,7 @@
     _, count, side, _ = master.shape
     shards = outers * reps
     plane = shards * cores
-    fetches = max(1, chips // shards)
-    limit = 0.25 * side * math.sqrt(count * plane * shards * fetches)
+    limit = 0.25 * side * math.sqrt(count * plane * plane)
     vmem = pl.BlockSpec(memory_space=pltpu.VMEM)
     smem = pl.BlockSpec(memory_space=pltpu.SMEM)
     hbm = pl.BlockSpec(memory_space=pl.ANY)
@@ -167,28 +166,25 @@
             out_specs=(vmem, vmem),
             compiler_params=small,
         )(first)
+        plane_sum = lax.psum(plane_sum, "core")
     later, plane_sum = lax.optimization_barrier((later, plane_sum))
     with jax.named_scope("later_slots"):
         later = lax.all_to_all(later, PEERS, 0, 0, tiled=True)
         later = later.reshape(shards * LATER, side, side)
     with jax.named_scope("z_shift"):
-        others = []
-        for k in range(fetches):
-            pairs = []
-            for o in range(outers):
-                for z in range(chips):
-                    for c in range(cores):
-                        for r in range(reps):
-                            p = o * reps + r
-                            away = k * shards // 2 + p // 2 + 1 if p % 2 else -(k * shards // 2 + p // 2)
-                            there = (z + away) % chips
-                            pairs.append(
-                                (((o * chips + z) * cores + c) * reps + r, ((o * chips + there) * cores + c) * reps + r)
-                            )
-            others.append(lax.ppermute(plane_sum, ALL, pairs))
-    others, later = lax.optimization_barrier((others, later))
+        pairs = []
+        for o in range(outers):
+            for z in range(chips):
+                for c in range(cores):
+                    for r in range(reps):
+                        there = (z + (o * cores + c) * reps + r - plane // 2 + 1) % chips
+                        pairs.append(
+                            (((o * chips + z) * cores + c) * reps + r, ((o * chips + there) * cores + c) * reps + r)
+                        )
+        other = lax.ppermute(plane_sum, ALL, pairs)
+    other, later = lax.optimization_barrier((other, later))
     with jax.named_scope("z_sum"):
-        sums = lax.all_to_all(jnp.broadcast_to(sum(others)[None], (plane, 8, TILE)), PLANE, 0, 0, tiled=True)
+        sums = lax.all_to_all(jnp.broadcast_to(other[None], (plane, 8, TILE)), PLANE, 0, 0, tiled=True)
     with jax.named_scope("apply"):
         return pl.pallas_call(
             functools.partial(apply_kernel, limit, count),

time: 89.6 us -> 79.1 us (0.88)
  blocking collectives: 52.7 us -> 42.2 us
  starting transfers between devices: 29 us -> 21.6 us
  waiting for transfers between devices: 0.07 us -> 7.35 us
    all_to_all x1, blocking collectives: 35.7 us -> 11.8 us  [body(): lax.all_to_all(jnp.broadcast_to(other[None], (plane, 8, TILE)), PLANE, 0,...]
    psum x0 -> x1, blocking collectives: none -> 13.4 us  [body(): plane_sum = lax.psum(plane_sum, 'core')]
    ppermute x2 -> x1, starting transfers between devices: 25.3 us -> 17.9 us  [body(): other = lax.ppermute(plane_sum, ALL, pairs)]
    all_to_all x1, waiting for transfers between devices: 0.01 us -> 6.61 us  [body(): later = lax.all_to_all(later, PEERS, 0, 0, tiled=True)]
  transfers between devices with their start and end apart: 3 -> 2, of which waited for: 1 -> 2; matrix products, arithmetic and copies ran while one was open for 0% -> 0% of each run, Pallas kernels for 0% -> 0%
where the time goes in v9:
time: 79.1 us; the launch traced here: 78.7 us
  blocking collectives  42.2 us (53%)
  starting transfers between devices  21.6 us (27%)
  Pallas kernels  7.54 us (10%)
  waiting for transfers between devices  7.35 us (9%)
    ppermute x1, starting transfers between devices, body(): other = lax.ppermute(plane_sum, ALL, pairs)  17.9 us
    all_to_all x1, blocking collectives, body(): first = lax.all_to_all(first, PEERS, 0, 0, tiled=True)  17 us
    psum x1, blocking collectives, body(): plane_sum = lax.psum(plane_sum, 'core')  13.4 us
    all_to_all x1, blocking collectives, body(): lax.all_to_all(jnp.broadcast_to(other[None], (plane, 8, TILE)), PLANE, 0,...  11.8 us
    all_to_all x1, waiting for transfers between devices, body(): later = lax.all_to_all(later, PEERS, 0, 0, tiled=True)  6.61 us
    pallas_call x1, Pallas kernels, body(): pl.pallas_call(functools.partial(apply_kernel, limit, count), out_shape=j...  4.7 us
    all_to_all x1, starting transfers between devices, body(): later = lax.all_to_all(later, PEERS, 0, 0, tiled=True)  3.71 us
    pallas_call x1, Pallas kernels, body(): pl.pallas_call(pick_kernel, out_shape=(jax.ShapeDtypeStruct((shards, side...  2.74 us
  transfers between devices with their start and end apart: 2, of which 2 were waited for; matrix products, arithmetic and copies ran while one was open for 0% of the time, Pallas kernels for 0%

profile of v9, /device:TPU:1, one launch (start us, length us, event | category | flops | bytes accessed | tf_op | source)
XLA Modules:
  0.0 78.7 jit_solution(15811362479868544616)
XLA Ops:
  0.0 2.7 %pick.1 = (bf16[16,144,128]{2,1,0:T(8,128)(2,1)}, bf16[16,3,128,128]{3,2,1,0:T(8,128)(2,1)}) custom-call(s32[1,7]{1,0:T(1,128)} %mask_hbm.1, f32[1,7,128,128]{3,2,1,0:T(8,128)} %master_hbm.1, bf16[1,7,128,128]{3,2,1,0:T(8,128)(2,1)} %synced_hbm.1), custom_call_target="tpu_custom_call" | custom-call | tf_op jit(solution)/shard_map/pick/pallas_call | solution.py:139
  2.8 17.0 %all_to_all.15.first_ref.first_hbm = bf16[16,144,128]{2,1,0:T(8,128)(2,1)S(1)} all-to-all(bf16[16,144,128]{2,1,0:T(8,128)(2,1)} %get-tuple-element.13), channel_id=1, replica_groups=mesh['outer'=4,'z'=32,'core'=2,'rep'=4] {'outer','rep'}, dimensions={0} | all-to-all | bytes 1179648 | tf_op jit(solution)/shard_map/first_slot/all_to_all | solution.py:158
  19.7 0.1 first_slot.1
  19.8 13.4 %psum.7 = f32[8,128]{1,0:T(8,128)S(1)} all-reduce(f32[8,128]{1,0:T(8,128)S(1)} %get-tuple-element.16), channel_id=1, replica_groups=mesh['outer'=4,'z'=32,'core'=2,'rep'=4] {'core'}, use_global_device_ids=true, to_apply=%region_0.0 | all-reduce | flops 1024 | bytes 8192 | tf_op jit(solution)/shard_map/first_slot/psum | solution.py:169
  33.2 3.7 %all-to-all-start.1 = ((bf16[16,3,128,128]{3,2,1,0:T(8,128)(2,1)}), bf16[16,3,128,128]{3,2,1,0:T(8,128)(2,1)S(1)}, u32[]{:S(2)}, u32[]{:S(2)}) async-start(bf16[16,3,128,128]{3,2,1,0:T(8,128)(2,1)} %get-tuple-element.18), calls=%async_computation.1 | async-start | bytes 3145728 | tf_op jit(solution)/shard_map/later_slots/all_to_all | solution.py:172
  36.9 17.9 %collective-permute-start = (f32[8,128]{1,0:T(8,128)S(1)}, f32[8,128]{1,0:T(8,128)S(1)}, u32[]{:S(2)}, u32[]{:S(2)}) collective-permute-start(f32[8,128]{1,0:T(8,128)S(1)} %psum.7), channel_id=1, source_target_pairs={{0,136},{1,145},{2,154},{3,163},{4,172},{5,181},{6,190},{7,199},{8... | collective-permute-start | bytes 12296 | tf_op jit(solution)/shard_map/z_shift/ppermute | solution.py:184
  54.8 0.7 collective-permute-done
  55.5 6.6 %all-to-all-done.1 = bf16[16,3,128,128]{3,2,1,0:T(8,128)(2,1)S(1)} async-done(((bf16[16,3,128,128]{3,2,1,0:T(8,128)(2,1)}), bf16[16,3,128,128]{3,2,1,0:T(8,128)(2,1)S(1)}, u32[]{:S(2)}, u32[]{:S(2)}) %all-to-all-start.1) | async-done | bytes 1572896 | tf_op jit(solution)/shard_map/later_slots/all_to_all | solution.py:172
  62.1 11.8 %all_to_all.16.sums_ref = f32[32,8,128]{2,1,0:T(8,128)S(1)} all-to-all(f32[32,8,128]{2,1,0:T(8,128)S(1)} %broadcast_in_dim.2), channel_id=1, replica_groups=mesh['outer'=4,'z'=32,'core'=2,'rep'=4] {'outer','core','rep'}, dimensions={0} | all-to-all | bytes 262144 | tf_op jit(solution)/shard_map/z_sum/all_to_all | solution.py:187
  74.0 4.7 %apply.1 = bf16[2,128,7168]{2,1,0:T(8,128)(2,1)} custom-call(s32[16,128]{1,0:T(8,128)S(1)} %get-tuple-element.14.table_ref, f32[32,8,128]{2,1,0:T(8,128)S(1)} %all_to_all.16.sums_ref, bf16[16,144,128]{2,1,0:T(8,128)(2,1)S(1)} %all_to_all.15.first_ref.first_hbm, bf16[48,128,128]{2,1,0:T(8,128)(2,1)S(1)} %bitcast.1, bf16[2,128,7168]{2,1,0:T(8,128)(2,1)} %resident_hbm.1), custom_call_target="tpu_custom_call" | custom-call | tf_op jit(solution)/shard_map/apply/pallas_call | solution.py:189
  (1 shorter events, 0.0 us)
Async XLA Ops:
  33.2 29.0 %all-to-all-start.1 = ((bf16[16,3,128,128]{3,2,1,0:T(8,128)(2,1)}), bf16[16,3,128,128]{3,2,1,0:T(8,128)(2,1)S(1)}, u32[]{:S(2)}, u32[]{:S(2)}) async-start(bf16[16,3,128,128]{3,2,1,0:T(8,128)(2,1)} %get-tuple-element.18), calls=%async_computation.1 | async-start | bytes 3145728 | tf_op jit(solution)/shard_map/later_slots/all_to_all | solution.py:172
  36.9 18.6 %collective-permute-start = (f32[8,128]{1,0:T(8,128)S(1)}, f32[8,128]{1,0:T(8,128)S(1)}, u32[]{:S(2)}, u32[]{:S(2)}) collective-permute-start(f32[8,128]{1,0:T(8,128)S(1)} %psum.7), channel_id=1, source_target_pairs={{0,136},{1,145},{2,154},{3,163},{4,172},{5,181},{6,190},{7,199},{8... | collective-permute-start | bytes 12296 | tf_op jit(solution)/shard_map/z_shift/ppermute | solution.py:184

commit v10 on v9

--- a/solution.py
+++ b/solution.py
@@ -81,7 +81,7 @@
 
 
 def apply_kernel(
-    limit, count, table_ref, sums_ref, first_hbm, later_ref, resident_hbm, out_hbm, rows_ref, first_ref, in_sem, first_sem, out_sem
+    limit, count, table_ref, sums_ref, first_ref, later_ref, resident_hbm, out_hbm, rows_ref, in_sem, out_sem
 ):
     shards = table_ref.shape[0]
     wide = count * TILE
@@ -91,17 +91,12 @@
         return ref.at[j // per_layer, :, pl.ds((j % per_layer) * wide, wide)]
 
     loads = [pltpu.make_async_copy(block(resident_hbm, j), block(rows_ref, j), in_sem.at[j]) for j in range(shards)]
-    firsts = [
-        pltpu.make_async_copy(first_hbm.at[j, pl.ds(0, TILE)], first_ref.at[j], first_sem.at[j]) for j in range(shards)
-    ]
     stores = [pltpu.make_async_copy(block(rows_ref, j), block(out_hbm, j), out_sem.at[j]) for j in range(shards)]
-    for first, load in zip(firsts, loads):
-        first.start()
+    for load in loads:
         load.start()
     total = jnp.sum(sums_ref[...], axis=0)
     factor = jnp.minimum(jnp.float32(1.0), limit / jnp.sqrt(total))[None]
     for j in range(shards):
-        firsts[j].wait()
         loads[j].wait()
 
         def add(slot, tile):
@@ -112,7 +107,7 @@
 
         @pl.when(table_ref[j, 1] > 0)
         def _():
-            add(0, first_ref[j])
+            add(0, first_ref[j, 0:TILE])
 
         def later(s, _):
             add(s, later_ref[j * LATER + s - 1])
@@ -166,7 +161,6 @@
             out_specs=(vmem, vmem),
             compiler_params=small,
         )(first)
-        plane_sum = lax.psum(plane_sum, "core")
     later, plane_sum = lax.optimization_barrier((later, plane_sum))
     with jax.named_scope("later_slots"):
         later = lax.all_to_all(later, PEERS, 0, 0, tiled=True)
@@ -181,7 +175,7 @@
                         pairs.append(
                             (((o * chips + z) * cores + c) * reps + r, ((o * chips + there) * cores + c) * reps + r)
                         )
-        other = lax.ppermute(plane_sum, ALL, pairs)
+        other = lax.ppermute(lax.psum(plane_sum, "core"), ALL, pairs)
     other, later = lax.optimization_barrier((other, later))
     with jax.named_scope("z_sum"):
         sums = lax.all_to_all(jnp.broadcast_to(other[None], (plane, 8, TILE)), PLANE, 0, 0, tiled=True)
@@ -189,12 +183,10 @@
         return pl.pallas_call(
             functools.partial(apply_kernel, limit, count),
             out_shape=jax.ShapeDtypeStruct(resident.shape, resident.dtype),
-            in_specs=[smem, vmem, hbm, vmem, hbm],
+            in_specs=[smem, vmem, vmem, vmem, hbm],
             out_specs=hbm,
             scratch_shapes=[
                 pltpu.VMEM(resident.shape, resident.dtype),
-                pltpu.VMEM((shards, side, side), jnp.bfloat16),
-                pltpu.SemaphoreType.DMA((shards,)),
                 pltpu.SemaphoreType.DMA((shards,)),
                 pltpu.SemaphoreType.DMA((shards,)),
             ],

time: 79.1 us -> 80.3 us (1.015)
  blocking collectives: 42.2 us -> 52.2 us
  waiting for transfers between devices: 7.35 us -> 0.74 us
  starting transfers between devices: 21.6 us -> 19.8 us
    all_to_all x1, blocking collectives: 11.8 us -> 20 us  [body(): lax.all_to_all(jnp.broadcast_to(other[None], (plane, 8, TILE)), PLANE, 0,...]
    all_to_all x1, waiting for transfers between devices: 6.61 us -> 0.01 us  [body(): later = lax.all_to_all(later, PEERS, 0, 0, tiled=True)]
    ppermute x1, starting transfers between devices: 17.9 us -> 16.1 us  [body(): other = lax.ppermute(lax.psum(plane_sum, 'core'), ALL, pairs)]
    psum x1, blocking collectives: 13.4 us -> 15.1 us  [body(): other = lax.ppermute(lax.psum(plane_sum, 'core'), ALL, pairs)]
  transfers between devices with their start and end apart: 2 -> 2, of which waited for: 2 -> 1; matrix products, arithmetic and copies ran while one was open for 0% -> 0% of each run, Pallas kernels for 0% -> 0%
where the time goes in v10:
time: 80.3 us; the launch traced here: 80 us
  blocking collectives  52.2 us (65%)
  starting transfers between devices  19.8 us (25%)
  Pallas kernels  7.21 us (9%)
    all_to_all x1, blocking collectives, body(): lax.all_to_all(jnp.broadcast_to(other[None], (plane, 8, TILE)), PLANE, 0,...  20 us
    all_to_all x1, blocking collectives, body(): first = lax.all_to_all(first, PEERS, 0, 0, tiled=True)  17 us
    ppermute x1, starting transfers between devices, body(): other = lax.ppermute(lax.psum(plane_sum, 'core'), ALL, pairs)  16.1 us
    psum x1, blocking collectives, body(): other = lax.ppermute(lax.psum(plane_sum, 'core'), ALL, pairs)  15.1 us
    pallas_call x1, Pallas kernels, body(): pl.pallas_call(functools.partial(apply_kernel, limit, count), out_shape=j...  4.38 us
    all_to_all x1, starting transfers between devices, body(): later = lax.all_to_all(later, PEERS, 0, 0, tiled=True)  3.72 us
    pallas_call x1, Pallas kernels, body(): pl.pallas_call(pick_kernel, out_shape=(jax.ShapeDtypeStruct((shards, side...  2.74 us
  transfers between devices with their start and end apart: 2, of which 1 were waited for; matrix products, arithmetic and copies ran while one was open for 0% of the time, Pallas kernels for 0%

profile of v10, /device:TPU:1, one launch (start us, length us, event | category | flops | bytes accessed | tf_op | source)
XLA Modules:
  0.0 80.0 jit_solution(5477587950864679410)
XLA Ops:
  0.0 2.7 %pick.1 = (bf16[16,144,128]{2,1,0:T(8,128)(2,1)}, bf16[16,3,128,128]{3,2,1,0:T(8,128)(2,1)}) custom-call(s32[1,7]{1,0:T(1,128)} %mask_hbm.1, f32[1,7,128,128]{3,2,1,0:T(8,128)} %master_hbm.1, bf16[1,7,128,128]{3,2,1,0:T(8,128)(2,1)} %synced_hbm.1), custom_call_target="tpu_custom_call" | custom-call | tf_op jit(solution)/shard_map/pick/pallas_call | solution.py:134
  2.8 17.0 %all_to_all.15.first_ref = bf16[16,144,128]{2,1,0:T(8,128)(2,1)S(1)} all-to-all(bf16[16,144,128]{2,1,0:T(8,128)(2,1)} %get-tuple-element.13), channel_id=1, replica_groups=mesh['outer'=4,'z'=32,'core'=2,'rep'=4] {'outer','rep'}, dimensions={0} | all-to-all | bytes 1179648 | tf_op jit(solution)/shard_map/first_slot/all_to_all | solution.py:153
  19.7 0.1 first_slot.1
  19.8 3.7 %all-to-all-start.1 = ((bf16[16,3,128,128]{3,2,1,0:T(8,128)(2,1)}), bf16[16,3,128,128]{3,2,1,0:T(8,128)(2,1)S(1)}, u32[]{:S(2)}, u32[]{:S(2)}) async-start(bf16[16,3,128,128]{3,2,1,0:T(8,128)(2,1)} %get-tuple-element.18), calls=%async_computation.1 | async-start | bytes 3145728 | tf_op jit(solution)/shard_map/later_slots/all_to_all | solution.py:166
  23.5 15.1 %psum.7 = f32[8,128]{1,0:T(8,128)S(1)} all-reduce(f32[8,128]{1,0:T(8,128)S(1)} %get-tuple-element.17), channel_id=1, replica_groups=mesh['outer'=4,'z'=32,'core'=2,'rep'=4] {'core'}, use_global_device_ids=true, to_apply=%region_0.0 | all-reduce | flops 1024 | bytes 8192 | tf_op jit(solution)/shard_map/z_shift/psum | solution.py:178
  38.7 16.1 %collective-permute-start = (f32[8,128]{1,0:T(8,128)S(1)}, f32[8,128]{1,0:T(8,128)S(1)}, u32[]{:S(2)}, u32[]{:S(2)}) collective-permute-start(f32[8,128]{1,0:T(8,128)S(1)} %psum.7), channel_id=1, source_target_pairs={{0,136},{1,145},{2,154},{3,163},{4,172},{5,181},{6,190},{7,199},{8... | collective-permute-start | bytes 12296 | tf_op jit(solution)/shard_map/z_shift/ppermute | solution.py:178
  54.8 0.7 collective-permute-done
  55.5 0.0 all-to-all-done.1
  55.5 20.0 %all_to_all.16.sums_ref = f32[32,8,128]{2,1,0:T(8,128)S(1)} all-to-all(f32[32,8,128]{2,1,0:T(8,128)S(1)} %broadcast_in_dim.2), channel_id=1, replica_groups=mesh['outer'=4,'z'=32,'core'=2,'rep'=4] {'outer','core','rep'}, dimensions={0} | all-to-all | bytes 262144 | tf_op jit(solution)/shard_map/z_sum/all_to_all | solution.py:181
  75.6 4.4 %apply.1 = bf16[2,128,7168]{2,1,0:T(8,128)(2,1)} custom-call(s32[16,128]{1,0:T(8,128)S(1)} %get-tuple-element.14.table_ref, f32[32,8,128]{2,1,0:T(8,128)S(1)} %all_to_all.16.sums_ref, bf16[16,144,128]{2,1,0:T(8,128)(2,1)S(1)} %all_to_all.15.first_ref, bf16[48,128,128]{2,1,0:T(8,128)(2,1)S(1)} %bitcast.1, bf16[2,128,7168]{2,1,0:T(8,128)(2,1)} %resident_hbm.1), custom_call_target="tpu_custom_call" | custom-call | tf_op jit(solution)/shard_map/apply/pallas_call | solution.py:183
  (1 shorter events, 0.0 us)
Async XLA Ops:
  19.8 35.7 %all-to-all-start.1 = ((bf16[16,3,128,128]{3,2,1,0:T(8,128)(2,1)}), bf16[16,3,128,128]{3,2,1,0:T(8,128)(2,1)S(1)}, u32[]{:S(2)}, u32[]{:S(2)}) async-start(bf16[16,3,128,128]{3,2,1,0:T(8,128)(2,1)} %get-tuple-element.18), calls=%async_computation.1 | async-start | bytes 3145728 | tf_op jit(solution)/shard_map/later_slots/all_to_all | solution.py:166
  38.7 16.8 %collective-permute-start = (f32[8,128]{1,0:T(8,128)S(1)}, f32[8,128]{1,0:T(8,128)S(1)}, u32[]{:S(2)}, u32[]{:S(2)}) collective-permute-start(f32[8,128]{1,0:T(8,128)S(1)} %psum.7), channel_id=1, source_target_pairs={{0,136},{1,145},{2,154},{3,163},{4,172},{5,181},{6,190},{7,199},{8... | collective-permute-start | bytes 12296 | tf_op jit(solution)/shard_map/z_shift/ppermute | solution.py:178

commit v11 on v10

--- a/solution.py
+++ b/solution.py
@@ -9,8 +9,9 @@
 from jax.sharding import Mesh, PartitionSpec as P
 
 SLOTS = 4
-LATER = SLOTS - 1
 TILE = 128
+EARLY = 64
+LATER = SLOTS * TILE - EARLY
 SMALL = 4 * 2**20
 LARGE = 53 * 10**6
 PICK = 568 * 10**5
@@ -44,9 +45,10 @@
     for s in range(SLOTS):
         delta = (master_ref[0, where[s]] - synced_ref[0, where[s]].astype(jnp.float32)).astype(jnp.bfloat16)
         if s == 0:
-            first_ref[0:TILE] = delta
+            first_ref[0:EARLY] = delta[0:EARLY]
+            later_ref[LATER - TILE + EARLY:LATER] = delta[EARLY:TILE]
         else:
-            later_ref[s - 1] = delta
+            later_ref[(s - 1) * TILE:s * TILE] = delta
         wide = jnp.where(used > s, delta.astype(jnp.float32), 0.0)
         squares = squares + jnp.sum((wide * wide).reshape(-1, 8, TILE), axis=0)
     sends = [pltpu.make_async_copy(later_ref, later_hbm.at[j], out_sem.at[0, j]) for j in range(shards)]
@@ -60,7 +62,7 @@
     note = jnp.where(lane == 0, high, jnp.where(lane == 8, middle, jnp.where(lane == 9, low, 0.0)))
     for k, entry in enumerate([used] + where):
         note = jnp.where(lane == 1 + k, entry.astype(jnp.float32), note)
-    first_ref[TILE:TILE + 16] = note.astype(jnp.bfloat16)
+    first_ref[EARLY:EARLY + 16] = note.astype(jnp.bfloat16)
     firsts = [pltpu.make_async_copy(first_ref, first_hbm.at[j], out_sem.at[1, j]) for j in range(shards)]
     for send in firsts:
         send.start()
@@ -74,7 +76,7 @@
     part = (lane == 0) | (lane == 8) | (lane == 9)
     total = jnp.zeros((16, TILE), jnp.float32)
     for j in range(shards):
-        note = first_ref[j, TILE:TILE + 16].astype(jnp.float32)
+        note = first_ref[j, EARLY:EARLY + 16].astype(jnp.float32)
         total = total + jnp.sum(jnp.where(part, note, 0.0), axis=1, keepdims=True)
         table_ref[j:j + 1, :] = jnp.where(part, 0.0, note)[0:1].astype(jnp.int32)
     sum_ref[...] = total[0:8]
@@ -107,10 +109,11 @@
 
         @pl.when(table_ref[j, 1] > 0)
         def _():
-            add(0, first_ref[j, 0:TILE])
+            rest = later_ref[j, LATER - TILE + EARLY:LATER]
+            add(0, jnp.concatenate([first_ref[j, 0:EARLY], rest], axis=0))
 
         def later(s, _):
-            add(s, later_ref[j * LATER + s - 1])
+            add(s, later_ref[j, pl.ds(pl.multiple_of((s - 1) * TILE, TILE), TILE)])
             return 0
 
         lax.fori_loop(1, table_ref[j, 1], later, 0)
@@ -134,8 +137,8 @@
         first, later = pl.pallas_call(
             pick_kernel,
             out_shape=(
-                jax.ShapeDtypeStruct((shards, side + 16, side), jnp.bfloat16),
-                jax.ShapeDtypeStruct((shards, LATER, side, side), jnp.bfloat16),
+                jax.ShapeDtypeStruct((shards, EARLY + 16, side), jnp.bfloat16),
+                jax.ShapeDtypeStruct((shards, LATER, side), jnp.bfloat16),
             ),
             in_specs=[hbm, hbm, hbm],
             out_specs=(hbm, hbm),
@@ -143,8 +146,8 @@
                 pltpu.SMEM(keep_mask.shape, keep_mask.dtype),
                 pltpu.VMEM(master.shape, master.dtype),
                 pltpu.VMEM(synced.shape, synced.dtype),
-                pltpu.VMEM((side + 16, side), jnp.bfloat16),
-                pltpu.VMEM((LATER, side, side), jnp.bfloat16),
+                pltpu.VMEM((EARLY + 16, side), jnp.bfloat16),
+                pltpu.VMEM((LATER, side), jnp.bfloat16),
                 pltpu.SemaphoreType.DMA((3,)),
                 pltpu.SemaphoreType.DMA((2, shards)),
             ],
@@ -164,7 +167,6 @@
     later, plane_sum = lax.optimization_barrier((later, plane_sum))
     with jax.named_scope("later_slots"):
         later = lax.all_to_all(later, PEERS, 0, 0, tiled=True)
-        later = later.reshape(shards * LATER, side, side)
     with jax.named_scope("z_shift"):
         pairs = []
         for o in range(outers):

time: 80.3 us -> 80.3 us (level)
  starting transfers between devices: 19.8 us -> 17.1 us
  waiting for transfers between devices: 0.74 us -> 2.41 us
  blocking collectives: 52.2 us -> 53.1 us
    ppermute x1, starting transfers between devices: 16.1 us -> 13.3 us  [body(): other = lax.ppermute(lax.psum(plane_sum, 'core'), ALL, pairs)]
    ppermute x1, waiting for transfers between devices: 0.73 us -> 2.41 us  [body(): other = lax.ppermute(lax.psum(plane_sum, 'core'), ALL, pairs)]
    all_to_all x1, blocking collectives: 17 us -> 15.5 us  [body(): first = lax.all_to_all(first, PEERS, 0, 0, tiled=True)]
    psum x1, blocking collectives: 15.1 us -> 16.5 us  [body(): other = lax.ppermute(lax.psum(plane_sum, 'core'), ALL, pairs)]
    all_to_all x1, blocking collectives: 20 us -> 21.1 us  [body(): lax.all_to_all(jnp.broadcast_to(other[None], (plane, 8, TILE)), PLANE, 0,...]
where the time goes in v11:
time: 80.3 us; the launch traced here: 80 us
  blocking collectives  53.1 us (66%)
  starting transfers between devices  17.1 us (21%)
  Pallas kernels  7.36 us (9%)
  waiting for transfers between devices  2.41 us (3%)
    all_to_all x1, blocking collectives, body(): lax.all_to_all(jnp.broadcast_to(other[None], (plane, 8, TILE)), PLANE, 0,...  21.1 us
    psum x1, blocking collectives, body(): other = lax.ppermute(lax.psum(plane_sum, 'core'), ALL, pairs)  16.5 us
    all_to_all x1, blocking collectives, body(): first = lax.all_to_all(first, PEERS, 0, 0, tiled=True)  15.5 us
    ppermute x1, starting transfers between devices, body(): other = lax.ppermute(lax.psum(plane_sum, 'core'), ALL, pairs)  13.3 us
    pallas_call x1, Pallas kernels, body(): pl.pallas_call(functools.partial(apply_kernel, limit, count), out_shape=j...  4.54 us
    all_to_all x1, starting transfers between devices, body(): later = lax.all_to_all(later, PEERS, 0, 0, tiled=True)  3.73 us
    pallas_call x1, Pallas kernels, body(): pl.pallas_call(pick_kernel, out_shape=(jax.ShapeDtypeStruct((shards, EARL...  2.73 us
    ppermute x1, waiting for transfers between devices, body(): other = lax.ppermute(lax.psum(plane_sum, 'core'), ALL, pairs)  2.41 us
  transfers between devices with their start and end apart: 2, of which 1 were waited for; matrix products, arithmetic and copies ran while one was open for 0% of the time, Pallas kernels for 0%

profile of v11, /device:TPU:1, one launch (start us, length us, event | category | flops | bytes accessed | tf_op | source)
XLA Modules:
  0.0 80.0 jit_solution(8206557132449969809)
XLA Ops:
  0.0 2.7 %pick.1 = (bf16[16,80,128]{2,1,0:T(8,128)(2,1)}, bf16[16,448,128]{2,1,0:T(8,128)(2,1)}) custom-call(s32[1,7]{1,0:T(1,128)} %mask_hbm.1, f32[1,7,128,128]{3,2,1,0:T(8,128)} %master_hbm.1, bf16[1,7,128,128]{3,2,1,0:T(8,128)(2,1)} %synced_hbm.1), custom_call_target="tpu_custom_call" | custom-call | tf_op jit(solution)/shard_map/pick/pallas_call | solution.py:137
  2.7 15.5 %all_to_all.15.first_ref = bf16[16,80,128]{2,1,0:T(8,128)(2,1)S(1)} all-to-all(bf16[16,80,128]{2,1,0:T(8,128)(2,1)} %get-tuple-element.13), channel_id=1, replica_groups=mesh['outer'=4,'z'=32,'core'=2,'rep'=4] {'outer','rep'}, dimensions={0} | all-to-all | bytes 655360 | tf_op jit(solution)/shard_map/first_slot/all_to_all | solution.py:156
  18.2 0.1 first_slot.1
  18.3 3.7 %all-to-all-start.1 = ((bf16[16,448,128]{2,1,0:T(8,128)(2,1)}), bf16[16,448,128]{2,1,0:T(8,128)(2,1)S(1)}, u32[]{:S(2)}, u32[]{:S(2)}) async-start(bf16[16,448,128]{2,1,0:T(8,128)(2,1)} %get-tuple-element.18), calls=%async_computation.1 | async-start | bytes 3670016 | tf_op jit(solution)/shard_map/later_slots/all_to_all | solution.py:169
  22.1 16.5 %psum.7 = f32[8,128]{1,0:T(8,128)S(1)} all-reduce(f32[8,128]{1,0:T(8,128)S(1)} %get-tuple-element.17), channel_id=1, replica_groups=mesh['outer'=4,'z'=32,'core'=2,'rep'=4] {'core'}, use_global_device_ids=true, to_apply=%region_0.0 | all-reduce | flops 1024 | bytes 8192 | tf_op jit(solution)/shard_map/z_shift/psum | solution.py:180
  38.6 13.3 %collective-permute-start = (f32[8,128]{1,0:T(8,128)S(1)}, f32[8,128]{1,0:T(8,128)S(1)}, u32[]{:S(2)}, u32[]{:S(2)}) collective-permute-start(f32[8,128]{1,0:T(8,128)S(1)} %psum.7), channel_id=1, source_target_pairs={{0,136},{1,145},{2,154},{3,163},{4,172},{5,181},{6,190},{7,199},{8... | collective-permute-start | bytes 12296 | tf_op jit(solution)/shard_map/z_shift/ppermute | solution.py:180
  51.9 2.4 %collective-permute-done = f32[8,128]{1,0:T(8,128)S(1)} collective-permute-done((f32[8,128]{1,0:T(8,128)S(1)}, f32[8,128]{1,0:T(8,128)S(1)}, u32[]{:S(2)}, u32[]{:S(2)}) %collective-permute-start) | collective-permute-done | bytes 4128 | tf_op jit(solution)/shard_map/z_shift/ppermute | solution.py:180
  54.3 0.0 all-to-all-done.1.later_ref
  54.3 21.1 %all_to_all.16.sums_ref = f32[32,8,128]{2,1,0:T(8,128)S(1)} all-to-all(f32[32,8,128]{2,1,0:T(8,128)S(1)} %broadcast_in_dim.2), channel_id=1, replica_groups=mesh['outer'=4,'z'=32,'core'=2,'rep'=4] {'outer','core','rep'}, dimensions={0} | all-to-all | bytes 262144 | tf_op jit(solution)/shard_map/z_sum/all_to_all | solution.py:183
  75.4 4.5 %apply.1 = bf16[2,128,7168]{2,1,0:T(8,128)(2,1)} custom-call(s32[16,128]{1,0:T(8,128)S(1)} %get-tuple-element.14.table_ref, f32[32,8,128]{2,1,0:T(8,128)S(1)} %all_to_all.16.sums_ref, bf16[16,80,128]{2,1,0:T(8,128)(2,1)S(1)} %all_to_all.15.first_ref, bf16[16,448,128]{2,1,0:T(8,128)(2,1)S(1)} %all-to-all-done.1.later_ref, bf16[2,128,7168]{2,1,0:T(8,128)(2,1)} %resident_hbm.1), custom_call_target="tpu_custom_call" | custom-call | tf_op jit(solution)/shard_map/apply/pallas_call | solution.py:185
  (1 shorter events, 0.0 us)
Async XLA Ops:
  18.3 36.0 %all-to-all-start.1 = ((bf16[16,448,128]{2,1,0:T(8,128)(2,1)}), bf16[16,448,128]{2,1,0:T(8,128)(2,1)S(1)}, u32[]{:S(2)}, u32[]{:S(2)}) async-start(bf16[16,448,128]{2,1,0:T(8,128)(2,1)} %get-tuple-element.18), calls=%async_computation.1 | async-start | bytes 3670016 | tf_op jit(solution)/shard_map/later_slots/all_to_all | solution.py:169
  38.6 15.8 %collective-permute-start = (f32[8,128]{1,0:T(8,128)S(1)}, f32[8,128]{1,0:T(8,128)S(1)}, u32[]{:S(2)}, u32[]{:S(2)}) collective-permute-start(f32[8,128]{1,0:T(8,128)S(1)} %psum.7), channel_id=1, source_target_pairs={{0,136},{1,145},{2,154},{3,163},{4,172},{5,181},{6,190},{7,199},{8... | collective-permute-start | bytes 12296 | tf_op jit(solution)/shard_map/z_shift/ppermute | solution.py:180

commit v12 on v10

--- a/solution.py
+++ b/solution.py
@@ -161,6 +161,7 @@
             out_specs=(vmem, vmem),
             compiler_params=small,
         )(first)
+        plane_sum = lax.psum(plane_sum, "core")
     later, plane_sum = lax.optimization_barrier((later, plane_sum))
     with jax.named_scope("later_slots"):
         later = lax.all_to_all(later, PEERS, 0, 0, tiled=True)
@@ -175,7 +176,7 @@
                         pairs.append(
                             (((o * chips + z) * cores + c) * reps + r, ((o * chips + there) * cores + c) * reps + r)
                         )
-        other = lax.ppermute(lax.psum(plane_sum, "core"), ALL, pairs)
+        other = lax.ppermute(plane_sum, ALL, pairs)
     other, later = lax.optimization_barrier((other, later))
     with jax.named_scope("z_sum"):
         sums = lax.all_to_all(jnp.broadcast_to(other[None], (plane, 8, TILE)), PLANE, 0, 0, tiled=True)

time: 80.3 us -> 78.8 us (0.981)
  blocking collectives: 52.2 us -> 42.2 us
  waiting for transfers between devices: 0.74 us -> 7.35 us
  starting transfers between devices: 19.8 us -> 21.6 us
    all_to_all x1, blocking collectives: 20 us -> 11.8 us  [body(): lax.all_to_all(jnp.broadcast_to(other[None], (plane, 8, TILE)), PLANE, 0,...]
    all_to_all x1, waiting for transfers between devices: 0.01 us -> 6.61 us  [body(): later = lax.all_to_all(later, PEERS, 0, 0, tiled=True)]
    ppermute x1, starting transfers between devices: 16.1 us -> 17.9 us  [body(): other = lax.ppermute(plane_sum, ALL, pairs)]
    psum x1, blocking collectives: 15.1 us -> 13.4 us  [body(): plane_sum = lax.psum(plane_sum, 'core')]
  transfers between devices with their start and end apart: 2 -> 2, of which waited for: 1 -> 2; matrix products, arithmetic and copies ran while one was open for 0% -> 0% of each run, Pallas kernels for 0% -> 0%
where the time goes in v12:
time: 78.8 us; the launch traced here: 78.3 us
  blocking collectives  42.2 us (54%)
  starting transfers between devices  21.6 us (27%)
  waiting for transfers between devices  7.35 us (9%)
  Pallas kernels  7.16 us (9%)
    ppermute x1, starting transfers between devices, body(): other = lax.ppermute(plane_sum, ALL, pairs)  17.9 us
    all_to_all x1, blocking collectives, body(): first = lax.all_to_all(first, PEERS, 0, 0, tiled=True)  17 us
    psum x1, blocking collectives, body(): plane_sum = lax.psum(plane_sum, 'core')  13.4 us
    all_to_all x1, blocking collectives, body(): lax.all_to_all(jnp.broadcast_to(other[None], (plane, 8, TILE)), PLANE, 0,...  11.8 us
    all_to_all x1, waiting for transfers between devices, body(): later = lax.all_to_all(later, PEERS, 0, 0, tiled=True)  6.61 us
    pallas_call x1, Pallas kernels, body(): pl.pallas_call(functools.partial(apply_kernel, limit, count), out_shape=j...  4.32 us
    all_to_all x1, starting transfers between devices, body(): later = lax.all_to_all(later, PEERS, 0, 0, tiled=True)  3.71 us
    pallas_call x1, Pallas kernels, body(): pl.pallas_call(pick_kernel, out_shape=(jax.ShapeDtypeStruct((shards, side...  2.74 us
  transfers between devices with their start and end apart: 2, of which 2 were waited for; matrix products, arithmetic and copies ran while one was open for 0% of the time, Pallas kernels for 0%

profile of v12, /device:TPU:1, one launch (start us, length us, event | category | flops | bytes accessed | tf_op | source)
XLA Modules:
  0.0 78.3 jit_solution(416624664359727108)
XLA Ops:
  0.0 2.7 %pick.1 = (bf16[16,144,128]{2,1,0:T(8,128)(2,1)}, bf16[16,3,128,128]{3,2,1,0:T(8,128)(2,1)}) custom-call(s32[1,7]{1,0:T(1,128)} %mask_hbm.1, f32[1,7,128,128]{3,2,1,0:T(8,128)} %master_hbm.1, bf16[1,7,128,128]{3,2,1,0:T(8,128)(2,1)} %synced_hbm.1), custom_call_target="tpu_custom_call" | custom-call | tf_op jit(solution)/shard_map/pick/pallas_call | solution.py:134
  2.8 17.0 %all_to_all.15.first_ref = bf16[16,144,128]{2,1,0:T(8,128)(2,1)S(1)} all-to-all(bf16[16,144,128]{2,1,0:T(8,128)(2,1)} %get-tuple-element.13), channel_id=1, replica_groups=mesh['outer'=4,'z'=32,'core'=2,'rep'=4] {'outer','rep'}, dimensions={0} | all-to-all | bytes 1179648 | tf_op jit(solution)/shard_map/first_slot/all_to_all | solution.py:153
  19.7 0.1 first_slot.1
  19.8 13.4 %psum.7 = f32[8,128]{1,0:T(8,128)S(1)} all-reduce(f32[8,128]{1,0:T(8,128)S(1)} %get-tuple-element.16), channel_id=1, replica_groups=mesh['outer'=4,'z'=32,'core'=2,'rep'=4] {'core'}, use_global_device_ids=true, to_apply=%region_0.0 | all-reduce | flops 1024 | bytes 8192 | tf_op jit(solution)/shard_map/first_slot/psum | solution.py:164
  33.2 3.7 %all-to-all-start.1 = ((bf16[16,3,128,128]{3,2,1,0:T(8,128)(2,1)}), bf16[16,3,128,128]{3,2,1,0:T(8,128)(2,1)S(1)}, u32[]{:S(2)}, u32[]{:S(2)}) async-start(bf16[16,3,128,128]{3,2,1,0:T(8,128)(2,1)} %get-tuple-element.18), calls=%async_computation.1 | async-start | bytes 3145728 | tf_op jit(solution)/shard_map/later_slots/all_to_all | solution.py:167
  36.9 17.9 %collective-permute-start = (f32[8,128]{1,0:T(8,128)S(1)}, f32[8,128]{1,0:T(8,128)S(1)}, u32[]{:S(2)}, u32[]{:S(2)}) collective-permute-start(f32[8,128]{1,0:T(8,128)S(1)} %psum.7), channel_id=1, source_target_pairs={{0,136},{1,145},{2,154},{3,163},{4,172},{5,181},{6,190},{7,199},{8... | collective-permute-start | bytes 12296 | tf_op jit(solution)/shard_map/z_shift/ppermute | solution.py:179
  54.8 0.7 collective-permute-done
  55.5 6.6 %all-to-all-done.1 = bf16[16,3,128,128]{3,2,1,0:T(8,128)(2,1)S(1)} async-done(((bf16[16,3,128,128]{3,2,1,0:T(8,128)(2,1)}), bf16[16,3,128,128]{3,2,1,0:T(8,128)(2,1)S(1)}, u32[]{:S(2)}, u32[]{:S(2)}) %all-to-all-start.1) | async-done | bytes 1572896 | tf_op jit(solution)/shard_map/later_slots/all_to_all | solution.py:167
  62.1 11.8 %all_to_all.16.sums_ref = f32[32,8,128]{2,1,0:T(8,128)S(1)} all-to-all(f32[32,8,128]{2,1,0:T(8,128)S(1)} %broadcast_in_dim.2), channel_id=1, replica_groups=mesh['outer'=4,'z'=32,'core'=2,'rep'=4] {'outer','core','rep'}, dimensions={0} | all-to-all | bytes 262144 | tf_op jit(solution)/shard_map/z_sum/all_to_all | solution.py:182
  74.0 4.3 %apply.1 = bf16[2,128,7168]{2,1,0:T(8,128)(2,1)} custom-call(s32[16,128]{1,0:T(8,128)S(1)} %get-tuple-element.14.table_ref, f32[32,8,128]{2,1,0:T(8,128)S(1)} %all_to_all.16.sums_ref, bf16[16,144,128]{2,1,0:T(8,128)(2,1)S(1)} %all_to_all.15.first_ref, bf16[48,128,128]{2,1,0:T(8,128)(2,1)S(1)} %bitcast.1, bf16[2,128,7168]{2,1,0:T(8,128)(2,1)} %resident_hbm.1), custom_call_target="tpu_custom_call" | custom-call | tf_op jit(solution)/shard_map/apply/pallas_call | solution.py:184
  (1 shorter events, 0.0 us)
Async XLA Ops:
  33.2 29.0 %all-to-all-start.1 = ((bf16[16,3,128,128]{3,2,1,0:T(8,128)(2,1)}), bf16[16,3,128,128]{3,2,1,0:T(8,128)(2,1)S(1)}, u32[]{:S(2)}, u32[]{:S(2)}) async-start(bf16[16,3,128,128]{3,2,1,0:T(8,128)(2,1)} %get-tuple-element.18), calls=%async_computation.1 | async-start | bytes 3145728 | tf_op jit(solution)/shard_map/later_slots/all_to_all | solution.py:167
  36.9 18.6 %collective-permute-start = (f32[8,128]{1,0:T(8,128)S(1)}, f32[8,128]{1,0:T(8,128)S(1)}, u32[]{:S(2)}, u32[]{:S(2)}) collective-permute-start(f32[8,128]{1,0:T(8,128)S(1)} %psum.7), channel_id=1, source_target_pairs={{0,136},{1,145},{2,154},{3,163},{4,172},{5,181},{6,190},{7,199},{8... | collective-permute-start | bytes 12296 | tf_op jit(solution)/shard_map/z_shift/ppermute | solution.py:179
